TPU v7x, 256 devices: a whole 4x4x8 slice. The times are simulated.
256 devices in a mesh: row: 8 (over y, z_lo), col: 16 (over z_hi, x), seq: 2 (over core).
Axes of the slice: x: 4, y: 4, z: 8 (z_hi: 4, z_lo: 2; z = z_hi * 2 + z_lo), core: 2. Of those that a mesh axis runs over, the one named last changes fastest.
Arguments:
- pair: float32 [256, 256, 128], P('row', ('col', 'seq')), may hold values from -6 to 6
- alignment_left: float32 [128, 256, 32], P('seq', 'row', 'col'), may hold values from -6 to 6
- alignment_right: float32 [128, 256, 32], P('seq', 'col', 'row'), may hold values from -6 to 6
- outer_mean_weight: float32 [1024, 128], replicated, may hold values from -4 to 4
- outer_mean_bias: float32 [128], replicated, may hold values from -192 to 192
- input_norm_gain: float32 [128], replicated, may hold values from 0.1 to 1.9
- input_norm_bias: float32 [128], replicated, may hold values from -4 to 4
- input_weight_matrix: float32 [128, 640], replicated, may hold values from -0.5 to 0.5
- input_bias_vector: float32 [640], replicated, may hold values from -4 to 4
- output_norm_gain: float32 [128], replicated, may hold values from 0.1 to 1.9
- output_norm_bias: float32 [128], replicated, may hold values from -4 to 4
- output_weight_matrix: float32 [128, 128], replicated, may hold values from -0.5 to 0.5
- output_bias_vector: float32 [128], replicated, may hold values from -4 to 4
Outputs:
- pair_out: float32 [256, 256, 128], P('row', ('col', 'seq'))
All inputs are finite; a program needn't handle non-finite values.
Results may differ from a plain program's by a relative error of at most 0.000064.
Values sent between devices are 32-bit elements; how exact they have to be, the bound alone decides.
No kernel may reach another device: no remote copies, remote signals or barrier semaphores. Data moves between devices by JAX's collectives and lax.ppermute only.
A program may use at most 64 MiB of HBM per device.

v0:
```python
import functools
import math

import jax
import jax.numpy as jnp
from jax import lax
from jax.sharding import PartitionSpec as P

SEQUENCE_COUNT = 128


highest = lax.Precision.HIGHEST


def from_root(value, axis, source):
    kept = jnp.where(lax.axis_index(axis) == source, value, 0).astype(value.dtype)
    return lax.psum(kept, axis)


def layer_norm(values, gain, shift):
    center = values - jnp.mean(values, axis=-1, keepdims=True)
    spread = jnp.mean(center * center, axis=-1, keepdims=True)
    return center * lax.rsqrt(spread + 1e-05) * gain + shift


def outer_block(left_block, right_flattened, outer_mean_weight):
    sequence_span, row_span, width_extent = left_block.shape
    column_span = right_flattened.shape[1] // width_extent
    outer = jnp.dot(
        left_block.reshape(sequence_span, row_span * width_extent).T,
        right_flattened,
        precision=highest,
    )
    outer = (
        outer.reshape(row_span, width_extent, column_span, width_extent)
        .transpose(0, 2, 1, 3)
        .reshape(row_span * column_span, width_extent * width_extent)
    )
    return jnp.dot(outer, outer_mean_weight, precision=highest).reshape(row_span, column_span, -1)


def per_device(
    pair,
    alignment_left,
    alignment_right,
    outer_mean_weight,
    outer_mean_bias,
    input_norm_gain,
    input_norm_bias,
    input_weight_matrix,
    input_bias_vector,
    output_norm_gain,
    output_norm_bias,
    output_weight_matrix,
    output_bias_vector,
):
    left_alignment = lax.all_gather(alignment_left, "col", axis=2, tiled=True)
    right_alignment = lax.all_gather(alignment_right, "row", axis=2, tiled=True)
    sequence_span, row_span, width_extent = left_alignment.shape
    column_span = right_alignment.shape[1]
    stride_amount = math.gcd(row_span, 16)
    block_list = left_alignment.reshape(
        sequence_span, row_span // stride_amount, stride_amount, width_extent
    ).transpose(1, 0, 2, 3)
    right_flattened = right_alignment.reshape(sequence_span, column_span * width_extent)
    partial_sum = lax.map(
        functools.partial(
            outer_block, right_flattened=right_flattened, outer_mean_weight=outer_mean_weight
        ),
        block_list,
    )
    partial_sum = partial_sum.reshape(row_span, column_span, -1)
    share = pair.shape[1]
    summed = lax.psum(partial_sum, "seq")
    summed = lax.dynamic_slice_in_dim(summed, lax.axis_index("seq") * share, share, 1)
    updated = pair + (summed + outer_mean_bias) / SEQUENCE_COUNT
    channels = pair.shape[2]
    normed = layer_norm(updated, input_norm_gain, input_norm_bias)
    proj = (
        jnp.dot(normed.reshape(-1, channels), input_weight_matrix, precision=highest)
        + input_bias_vector
    )
    left_act = (jax.nn.sigmoid(proj[:, channels : 2 * channels]) * proj[:, :channels]).reshape(
        pair.shape
    )
    right_act = (
        jax.nn.sigmoid(proj[:, 3 * channels : 4 * channels]) * proj[:, 2 * channels : 3 * channels]
    ).reshape(pair.shape)
    gate = jax.nn.sigmoid(proj[:, 4 * channels :]).reshape(pair.shape)
    right_panel = lax.all_gather(right_act, "row", axis=0, tiled=True)
    row_count = lax.axis_size("row")
    ratio = lax.axis_size(("col", "seq")) // row_count
    columns = lax.all_gather(left_act, "row", axis=0, tiled=True)
    base = lax.axis_index("row") * ratio
    pieces = []
    for offset in range(ratio):
        owned = from_root(columns, ("col", "seq"), base + offset)
        pieces.append(jnp.einsum("kic,kjc->ijc", owned, right_panel, precision=highest))
    mixed = jnp.concatenate(pieces, axis=0)
    normed_out = layer_norm(mixed, output_norm_gain, output_norm_bias)
    result = (
        jnp.dot(normed_out.reshape(-1, channels), output_weight_matrix, precision=highest)
        + output_bias_vector
    )
    return updated + gate * result.reshape(pair.shape)


def solution(mesh):
    return jax.shard_map(
        per_device,
        mesh=mesh,
        in_specs=(
            P("row", ("col", "seq"), None),
            P("seq", "row", "col"),
            P("seq", "col", "row"),
            P(),
            P(),
            P(),
            P(),
            P(),
            P(),
            P(),
            P(),
            P(),
            P(),
        ),
        out_specs=P("row", ("col", "seq"), None),
        check_vma=False,
    )
```

profile of v0, /device:TPU:1, one launch (start us, length us, event | category | flops | bytes accessed | tf_op | source)
XLA Modules:
  0.0 544.1 jit_solution(1551249813458931231)
XLA Ops:
  6.5 0.8 copy.87
  7.3 44.0 %all_gather.12 = f32[64,32,32]{0,1,2:T(8,128)S(1)} all-gather(f32[64,32,2]{0,1,2:T(8,128)S(1)} %copy.87), channel_id=1, replica_groups=mesh['row'=8,'col'=16,'seq'=2] {'col'}, dimensions={2}, use_global_device_ids=true | all-gather | bytes 278528 | tf_op jit(solution)/shard_map/all_gather | solution.py:57
  52.4 22.9 %all_gather.13 = f32[64,16,32]{0,1,2:T(8,128)S(1)} all-gather(f32[64,16,4]{0,1,2:T(8,128)S(1)} %copy.89), channel_id=1, replica_groups=mesh['row'=8,'col'=16,'seq'=2] {'row'}, dimensions={2}, use_global_device_ids=true | all-gather | bytes 147456 | tf_op jit(solution)/shard_map/all_gather | solution.py:58
  75.5 19.7 %while.10 = (s32[]{:T(128)}, f32[2,16,16,128]{3,2,1,0:T(8,128)S(1)}, f32[2,64,16,32]{1,3,2,0:T(8,128)S(1)}, f32[64,512]{0,1:T(8,128)S(1)}, f32[1024,128]{1,0:T(8,128)}, /*index=5*/s32[]{:T(128)}) while((s32[]{:T(128)}, f32[2,16,16,128]{3,2,1,0:T(8,128)S(1)}, f32[2,64,16,32]{1,3,2,0:T(8,128)S(1)}, f32[64,512]{0,1:T(8,128)S(1)}, ...), condition=%wide.region_1.2_spmd, body=%wide.region_0.1_spmd.sunk | while | flops 603979776 | bytes 7471209 | solution.py:66
  75.5 5.0 convolution_bitcast_fusion.7
  80.5 3.7 reshape.94
  84.3 1.0 fusion.59
  85.3 5.0 convolution_bitcast_fusion.7
  90.3 3.7 reshape.94
  94.1 1.0 fusion.59
  95.9 36.9 %all-reduce.4.cloned.1.call-done = f32[32,16,128]{2,1,0:T(8,128)} async-done(((f32[32,16,128]{2,1,0:T(8,128)}), f32[32,16,128]{2,1,0:T(8,128)}) %all-reduce.4.cloned.1.call-update) | async-done | bytes 262160 | tf_op jit(solution)/shard_map/psum | solution.py:74
  132.8 1.0 fusion.37
  134.8 0.8 fusion.8
  136.6 38.2 %all-gather.5.cloned.1.call-done = f32[256,8,128]{2,1,0:T(8,128)} async-done(((f32[32,8,128]{2,1,0:T(8,128)}), f32[256,8,128]{2,1,0:T(8,128)}) %all-gather.5.cloned.1.call-update) | async-done | bytes 1048592 | tf_op jit(solution)/shard_map/all_gather | solution.py:93
  174.9 1.7 copy.91
  176.6 2.1 broadcast_select_fusion.3
  178.7 40.1 %all-gather.3.cloned.1.call-done = f32[256,8,128]{2,1,0:T(8,128)} async-done(((f32[32,8,128]{2,1,0:T(8,128)}), f32[256,8,128]{2,1,0:T(8,128)}) %all-gather.3.cloned.1.call-update) | async-done | bytes 1048592 | tf_op jit(solution)/shard_map/all_gather | solution.py:90
  218.8 1.7 copy.92
  220.5 307.9 %all-reduce.6.cloned.1.call-done = (f32[256,8,128]{0,1,2:T(8,128)}, f32[256,8,128]{0,1,2:T(8,128)}, f32[256,8,128]{0,1,2:T(8,128)}, f32[256,8,128]{0,1,2:T(8,128)}) async-done(((f32[256,8,128]{0,1,2:T(8,128)}, f32[256,8,128]{0,1,2:T(8,128)}, f32[256,8,128]{0,1,2:T(8,128)}, f32[256,8,128]{0,1,2:T(8,128)}), (f32[256,8,128]{0,1,2:T(8,128)}, f32[256,8,128]{0,1,2:T(8,128)}, f32[256,8,128]{0,1,2:T(8,128)}, ...) | async-done | bytes 4194320 | tf_op jit(solution)/shard_map/psum | solution.py:17
  528.4 2.4 convolution_bitcast_fusion.5
  530.8 2.3 convolution_bitcast_fusion.4
  533.2 1.0 convolution_bitcast_fusion.3
  534.2 1.0 convolution_bitcast_fusion.2
  536.6 1.0 fusion.7
  (56 shorter events, 5.1 us)
Async XLA Ops:
  6.5 127.5 %copy-start = (f32[128,640]{1,0:T(8,128)S(1)}, f32[128,640]{1,0:T(8,128)}, u32[]{:S(2)}) copy-start(f32[128,640]{1,0:T(8,128)} %param.22) | copy-start | bytes 983044
  6.5 126.3 %all-reduce.4.cloned.1.call-start = ((), (), s32[]{:S(2)}) async-start(), calls=%async_computation | async-start | bytes 524288 | tf_op jit(solution)/shard_map/psum | solution.py:74
  75.4 57.4 %copy-start.5 = (f32[32,8,128]{2,1,0:T(8,128)S(1)}, f32[32,8,128]{2,1,0:T(8,128)}, u32[]{:S(2)}) copy-start(f32[32,8,128]{2,1,0:T(8,128)} %param.15) | copy-start | bytes 393220
  75.4 57.4 %copy-start.7 = (f32[128]{0:T(128)S(1)}, f32[128]{0:T(128)}, u32[]{:S(2)}) copy-start(f32[128]{0:T(128)} %param.19) | copy-start | bytes 1540
  75.4 58.7 %copy-start.6 = (f32[640]{0:T(1024)S(1)}, f32[640]{0:T(1024)}, u32[]{:S(2)}) copy-start(f32[640]{0:T(1024)} %param.23) | copy-start | bytes 7684
  75.4 58.7 %copy-start.8 = (f32[128]{0:T(128)S(1)}, f32[128]{0:T(128)}, u32[]{:S(2)}) copy-start(f32[128]{0:T(128)} %param.21) | copy-start | bytes 1540
  75.4 58.7 %copy-start.9 = (f32[128]{0:T(128)S(1)}, f32[128]{0:T(128)}, u32[]{:S(2)}) copy-start(f32[128]{0:T(128)} %param.20) | copy-start | bytes 1540
  75.5 8.8 %copy-start.1 = (f32[1024,128]{1,0:T(8,128)S(1)}, f32[1024,128]{1,0:T(8,128)}, u32[]{:S(2)}) copy-start(f32[1024,128]{1,0:T(8,128)} %get-tuple-element.104) | copy-start | bytes 1572868 | tf_op jit(solution)/shard_map/while
  85.3 8.8 %copy-start.1 = (f32[1024,128]{1,0:T(8,128)S(1)}, f32[1024,128]{1,0:T(8,128)}, u32[]{:S(2)}) copy-start(f32[1024,128]{1,0:T(8,128)} %get-tuple-element.104) | copy-start | bytes 1572868 | tf_op jit(solution)/shard_map/while
  95.1 0.7 copy-start.4
  95.8 79.0 %all-gather.5.cloned.1.call-start = ((), (), s32[]{:S(2)}) async-start(), calls=%async_computation.2 | async-start | bytes 1179648 | tf_op jit(solution)/shard_map/all_gather | solution.py:93
  135.6 83.2 %all-gather.3.cloned.1.call-start = ((), (), s32[]{:S(2)}) async-start(), calls=%async_computation.1 | async-start | bytes 1179648 | tf_op jit(solution)/shard_map/all_gather | solution.py:90
  136.4 392.0 %all-reduce.6.cloned.1.call-start = ((), (), s32[]{:S(2)}) async-start(), calls=%async_computation.3 | async-start | bytes 8388608 | tf_op jit(solution)/shard_map/psum | solution.py:17
  528.4 4.7 copy-start.3
  528.4 5.8 %copy-start.2 = (f32[256,8,128]{0,1,2:T(8,128)S(1)}, f32[256,8,128]{0,1,2:T(8,128)}, u32[]{:S(2)}) copy-start(f32[256,8,128]{0,1,2:T(8,128)} %get-tuple-element.43) | copy-start | bytes 3145732
  533.1 3.5 copy-start.10
  533.1 3.4 copy-start.11
  533.1 3.4 copy-start.12
  533.2 3.4 copy-start.13
Sparse Core Ops, SparseCore 0:
  96.0 36.8 all-reduce.3
  135.8 39.0 all-gather.4
  176.8 41.9 all-gather.2
  221.8 306.5 all-reduce.5
where the time goes:
time: 545 us; the launch traced here: 544 us
  waiting for transfers between devices  424 us (78%)
  blocking collectives  66.9 us (12%)
  matrix products  20.5 us (4%)
  local copies, waits for them, and re-layouts  14.3 us (3%)
  between operations  13.4 us (2%)
    psum x1, waiting for transfers between devices, from_root(): return lax.psum(kept, axis)  308 us
    all_gather x1, blocking collectives, per_device(): left_alignment = lax.all_gather(alignment_left, 'col', axis=2, tiled=True)  44 us
    all_gather x1, waiting for transfers between devices, per_device(): right_panel = lax.all_gather(right_act, 'row', axis=0, tiled=True)  40.1 us
    all_gather x1, waiting for transfers between devices, per_device(): columns = lax.all_gather(left_act, 'row', axis=0, tiled=True)  38.2 us
    psum x1, waiting for transfers between devices, per_device(): summed = lax.psum(partial_sum, 'seq')  36.9 us
    all_gather x1, blocking collectives, per_device(): right_alignment = lax.all_gather(alignment_right, 'row', axis=2, tiled=True)  22.9 us
  transfers between devices with their start and end apart: 4, of which 4 were waited for; matrix products, arithmetic and copies ran while one was open for 1% of the time, Pallas kernels for 0%

commit v1 on v0

v1 whole, which is shorter than its diff:
```python
import functools

import jax
import jax.numpy as jnp
from jax import lax
from jax.experimental import pallas as pl
from jax.experimental.pallas import tpu as pltpu
from jax.sharding import PartitionSpec as P

SEQUENCE_COUNT = 128
EPSILON = 1e-05
LANES = 128
VMEM_LIMIT = 32 * 1024 * 1024


def split(value):
    high = value.astype(jnp.bfloat16)
    return high, (value - high.astype(jnp.float32)).astype(jnp.bfloat16)


def product(left, right, transposed):
    dims = (((1,), (1 if transposed else 0,)), ((), ()))
    dot = functools.partial(
        lax.dot_general, dimension_numbers=dims, preferred_element_type=jnp.float32
    )
    return dot(left[0], right[0]) + (dot(left[0], right[1]) + dot(left[1], right[0]))


def swap_groups(blocks):
    lane = lax.broadcasted_iota(jnp.int32, blocks[0].shape, 1)
    wide, narrow = (lane & 64) == 0, (lane & 32) == 0

    def exchange(first, second, shift, mask):
        return (
            jnp.where(mask, first, pltpu.roll(second, shift, 1)),
            jnp.where(mask, pltpu.roll(first, LANES - shift, 1), second),
        )

    a, c = exchange(blocks[0], blocks[2], 64, wide)
    b, d = exchange(blocks[1], blocks[3], 64, wide)
    a, b = exchange(a, b, 32, narrow)
    c, d = exchange(c, d, 32, narrow)
    return a, b, c, d


def tile_kernel(
    row_ref,
    own_ref,
    other_ref,
    right_ref,
    pair_ref,
    mean_weight_ref,
    mean_bias_ref,
    gain_ref,
    shift_ref,
    weight_ref,
    send_ref,
    updated_ref,
    gate_ref,
    right_scratch,
    high_scratch,
    low_scratch,
):
    row = row_ref[0]
    for step in range(8):
        place = pl.multiple_of((row ^ step) * 32, 32)
        right_scratch[pl.ds(place, 32), :] = right_ref[step]
    right = split(
        jnp.concatenate([right_scratch[pl.ds(j, 32, stride=8), :] for j in range(8)], axis=0)
    )
    own, other = own_ref[...], other_ref[...]
    first_half = lax.broadcasted_iota(jnp.int32, own.shape, 1) < 64
    halves = (
        jnp.where(first_half, own, pltpu.roll(other, 64, 1)),
        jnp.where(first_half, pltpu.roll(own, 64, 1), other),
    )
    for half in range(2):
        outer = product(split(halves[half]), right, True)
        for wide in range(2):
            for group in range(8):
                blocks = [
                    outer[
                        (group * 4 + p) * 16 : (group * 4 + p + 1) * 16,
                        wide * LANES : (wide + 1) * LANES,
                    ]
                    for p in range(4)
                ]
                for j, block in enumerate(swap_groups(blocks)):
                    rows = pl.ds((wide * 4 + j) * 32 + half * 16, 16)
                    columns = pl.ds(group * LANES, LANES)
                    high, low = split(block)
                    high_scratch[rows, columns] = high
                    low_scratch[rows, columns] = low
    summed = product(
        (high_scratch[...], low_scratch[...]), split(mean_weight_ref[...]), False
    )
    pair = jnp.concatenate([pair_ref[pl.ds(j, 32, stride=8), :] for j in range(8)], axis=0)
    updated = pair + (summed + mean_bias_ref[...]) * (1.0 / SEQUENCE_COUNT)
    updated_ref[...] = updated
    center = updated - jnp.mean(updated, axis=1, keepdims=True)
    spread = jnp.mean(center * center, axis=1, keepdims=True)
    normed = center * lax.rsqrt(spread + EPSILON) * gain_ref[...] + shift_ref[...]
    one = (lax.broadcasted_iota(jnp.int32, normed.shape, 1) == 0).astype(jnp.float32)
    proj = product(split(weight_ref[...]), split(jnp.concatenate([normed, one], axis=1)), True)
    blocks = [proj[n * LANES : (n + 1) * LANES] for n in range(5)]
    left_act = jax.nn.sigmoid(blocks[1]) * blocks[0]
    right_act = jax.nn.sigmoid(blocks[3]) * blocks[2]
    send_ref[pl.ds(0, 128, stride=4), :] = left_act[:, :LANES]
    send_ref[pl.ds(1, 128, stride=4), :] = left_act[:, LANES:]
    send_ref[pl.ds(2, 128, stride=4), :] = right_act[:, :LANES]
    send_ref[pl.ds(3, 128, stride=4), :] = right_act[:, LANES:]
    gate_ref[...] = jax.nn.sigmoid(blocks[4])


def triangle_kernel(core_ref, own_ref, other_ref, send_ref, left_scratch, right_scratch):
    first_core = core_ref[0] == 0

    def regroup(source, part, wide):
        return swap_groups([source(wide * 4 + r, part) for r in range(4)])

    def rows_of(ref):
        return lambda r, part: ref[pl.ds(r * 64 + part, 16, stride=4), :]

    own, other = rows_of(own_ref), rows_of(other_ref)

    def lower(r, part):
        return jnp.where(first_core, own(r, part), other(r, part))

    def upper(r, part):
        return jnp.where(first_core, other(r, part), own(r, part))

    for wide in range(2):
        for part in range(2):
            for core, source in enumerate((lower, upper)):
                for g, block in enumerate(regroup(source, part, wide)):
                    place = core * 8 + part * 4 + g
                    left_scratch[wide, pl.ds(place, 16, stride=16), :] = block
            for g, block in enumerate(regroup(own, part + 2, wide)):
                right_scratch[wide, pl.ds((part * 4 + g) * 16, 16), :] = block
    left = split(jnp.concatenate([left_scratch[0], left_scratch[1]], axis=1))
    right = split(jnp.concatenate([right_scratch[0], right_scratch[1]], axis=1))
    mixed = product(right, left, True)
    for wide in range(2):
        for part in range(2):
            blocks = [
                mixed[
                    (part * 4 + g) * 16 : (part * 4 + g + 1) * 16,
                    wide * LANES : (wide + 1) * LANES,
                ]
                for g in range(4)
            ]
            for r, block in enumerate(swap_groups(blocks)):
                send_ref[pl.ds((wide * 4 + r) * 32 + part, 16, stride=2), :] = block


def output_kernel(mixed_ref, updated_ref, gate_ref, gain_ref, shift_ref, weight_ref, out_ref):
    mixed = jnp.concatenate(
        [mixed_ref[pl.ds(0, 128, stride=2), :], mixed_ref[pl.ds(1, 128, stride=2), :]], axis=1
    )
    center = mixed - jnp.mean(mixed, axis=0, keepdims=True)
    spread = jnp.mean(center * center, axis=0, keepdims=True)
    normed = center * lax.rsqrt(spread + EPSILON)
    weight = weight_ref[:, :LANES]
    bias = jnp.sum(weight * shift_ref[...], axis=1, keepdims=True) + weight_ref[:, LANES : LANES + 1]
    result = product(split(weight * gain_ref[...]), split(normed), False) + bias
    gated = jnp.transpose(gate_ref[...] * result)
    out = updated_ref[...] + gated
    for j in range(8):
        out_ref[pl.ds(j, 32, stride=8), :] = out[j * 32 : (j + 1) * 32]


def call(kernel, outputs, scratch, scalars, *operands):
    specs = [pl.BlockSpec(memory_space=pltpu.SMEM)] * scalars
    specs += [pl.BlockSpec(memory_space=pltpu.VMEM)] * (len(operands) - scalars)
    return pl.pallas_call(
        kernel,
        out_shape=[jax.ShapeDtypeStruct(shape, jnp.float32) for shape in outputs],
        in_specs=specs,
        out_specs=[pl.BlockSpec(memory_space=pltpu.VMEM)] * len(outputs),
        scratch_shapes=scratch,
        compiler_params=pltpu.CompilerParams(vmem_limit_bytes=VMEM_LIMIT),
    )(*operands)


def exchange(value, axis, distance):
    count = lax.axis_size(axis)
    return lax.ppermute(value, axis, [(n, n ^ distance) for n in range(count)])


def with_bias(weight, bias):
    rows = jnp.zeros((LANES, weight.shape[1]), jnp.float32).at[0].set(bias)
    return jnp.concatenate([weight, rows], axis=0).T


def per_device(
    pair,
    alignment_left,
    alignment_right,
    outer_mean_weight,
    outer_mean_bias,
    input_norm_gain,
    input_norm_bias,
    input_weight_matrix,
    input_bias_vector,
    output_norm_gain,
    output_norm_bias,
    output_weight_matrix,
    output_bias_vector,
):
    row, core = lax.axis_index("row"), lax.axis_index("seq")
    columns = alignment_right.transpose(2, 1, 0)
    mine = lax.dynamic_slice_in_dim(columns, core * 8, 8, 1)
    theirs = lax.dynamic_slice_in_dim(columns, (1 - core) * 8, 8, 1)
    right = jnp.concatenate([mine, exchange(theirs, "seq", 1)], axis=2).reshape(1, 32, LANES)
    for distance in (1, 2, 4):
        right = jnp.concatenate([right, exchange(right, "row", distance)], axis=0)
    left = alignment_left.transpose(2, 1, 0).reshape(2, 2, 16, 64)
    left = left.transpose(0, 2, 1, 3).reshape(1, 32, LANES)
    left = jnp.broadcast_to(left, (16, 32, LANES)).reshape(512, LANES)
    own = lax.all_to_all(left, "col", 0, 0, tiled=True)
    other = exchange(own, "seq", 1)
    send, updated, gate = call(
        tile_kernel,
        [(512, LANES), (256, LANES), (LANES, 256)],
        [
            pltpu.VMEM((256, LANES), jnp.float32),
            pltpu.VMEM((256, 1024), jnp.bfloat16),
            pltpu.VMEM((256, 1024), jnp.bfloat16),
        ],
        1,
        row.reshape(1),
        own,
        other,
        right,
        pair.reshape(256, LANES),
        outer_mean_weight,
        outer_mean_bias.reshape(1, LANES),
        input_norm_gain.reshape(1, LANES),
        input_norm_bias.reshape(1, LANES),
        with_bias(input_weight_matrix, input_bias_vector),
    )
    own = lax.all_to_all(send, ("row", "col"), 0, 0, tiled=True)
    other = exchange(own, "seq", 1)
    (back,) = call(
        triangle_kernel,
        [(256, LANES)],
        [
            pltpu.VMEM((2, 256, LANES), jnp.float32),
            pltpu.VMEM((2, 128, LANES), jnp.float32),
        ],
        1,
        core.reshape(1),
        own,
        other,
    )
    mixed = lax.all_to_all(back, ("row", "col"), 0, 0, tiled=True)
    (out,) = call(
        output_kernel,
        [(256, LANES)],
        [],
        0,
        mixed,
        updated,
        gate,
        output_norm_gain.reshape(1, LANES),
        output_norm_bias.reshape(1, LANES),
        with_bias(output_weight_matrix, output_bias_vector),
    )
    return out.reshape(pair.shape)


def solution(mesh):
    return jax.shard_map(
        per_device,
        mesh=mesh,
        in_specs=(
            P("row", ("col", "seq"), None),
            P("seq", "row", "col"),
            P("seq", "col", "row"),
            P(),
            P(),
            P(),
            P(),
            P(),
            P(),
            P(),
            P(),
            P(),
            P(),
        ),
        out_specs=P("row", ("col", "seq"), None),
        check_vma=False,
    )
```

time: 545 us -> 84.1 us (0.15)
  waiting for transfers between devices: 424 us -> 20 us
  blocking collectives: 66.9 us -> 21.8 us
  starting transfers between devices: 0.3 us -> 32.2 us
  matrix products: 20.5 us -> 0 us
  between operations: 13.4 us -> 0.18 us
  local copies, waits for them, and re-layouts: 14.3 us -> 4.69 us
    psum x2 -> x0, waiting for transfers between devices: 345 us -> none  [the longest x1 308 us: from_root(): return lax.psum(kept, axis)]
    all_gather x2 -> x0, waiting for transfers between devices: 78.3 us -> none  [the longest x1 40.1 us: per_device(): right_panel = lax.all_gather(right_act, 'row', axis=0, tiled=True)]
    all_gather x2 -> x0, blocking collectives: 66.9 us -> none  [the longest x1 44 us: per_device(): left_alignment = lax.all_gather(alignment_left, 'col', axis=2, tiled=True)]
    all_to_all x0 -> x1, blocking collectives: none -> 21.8 us  [per_device(): own = lax.all_to_all(send, ('row', 'col'), 0, 0, tiled=True)]
    dot_general x10 -> x0, matrix products: 20.5 us -> none  [the longest x2 10.1 us: outer_block(): jnp.dot(left_block.reshape(sequence_span, row_span * width_extent).T, rig...]
    all_to_all x0 -> x2, starting transfers between devices: none -> 18 us  [the longest x1 11.7 us: per_device(): own = lax.all_to_all(left, 'col', 0, 0, tiled=True)]
    ppermute x0 -> x6, starting transfers between devices: none -> 14.2 us  [exchange(): return lax.ppermute(value, axis, [(n, n ^ distance) for n in range(count)])]
    all_to_all x0 -> x2, waiting for transfers between devices: none -> 13.1 us  [the longest x1 10.5 us: per_device(): mixed = lax.all_to_all(back, ('row', 'col'), 0, 0, tiled=True)]
  transfers between devices with their start and end apart: 4 -> 8, of which waited for: 4 -> 6; matrix products, arithmetic and copies ran while one was open for 1% -> 1% of each run, Pallas kernels for 0% -> 0%
where the time goes in v1:
time: 84.1 us; the launch traced here: 83.6 us
  starting transfers between devices  32.2 us (38%)
  blocking collectives  21.8 us (26%)
  waiting for transfers between devices  20 us (24%)
  local copies, waits for them, and re-layouts  4.69 us (6%)
  Pallas kernels  4.62 us (5%)
    all_to_all x1, blocking collectives, per_device(): own = lax.all_to_all(send, ('row', 'col'), 0, 0, tiled=True)  21.8 us
    ppermute x6, starting transfers between devices, exchange(): return lax.ppermute(value, axis, [(n, n ^ distance) for n in range(count)])  14.2 us
    all_to_all x1, starting transfers between devices, per_device(): own = lax.all_to_all(left, 'col', 0, 0, tiled=True)  11.7 us
    all_to_all x1, waiting for transfers between devices, per_device(): mixed = lax.all_to_all(back, ('row', 'col'), 0, 0, tiled=True)  10.5 us
    ppermute x6, waiting for transfers between devices, exchange(): return lax.ppermute(value, axis, [(n, n ^ distance) for n in range(count)])  6.93 us
    all_to_all x1, starting transfers between devices, per_device(): mixed = lax.all_to_all(back, ('row', 'col'), 0, 0, tiled=True)  6.3 us
    pallas_call x3, Pallas kernels, call(): pl.pallas_call(kernel, out_shape=[jax.ShapeDtypeStruct(shape, jnp.float32...  4.62 us
    unnamed x26, local copies, waits for them, and re-layouts  2.82 us
  transfers between devices with their start and end apart: 8, of which 6 were waited for; matrix products, arithmetic and copies ran while one was open for 1% of the time, Pallas kernels for 0%

profile of v1, /device:TPU:1, one launch (start us, length us, event | category | flops | bytes accessed | tf_op | source)
XLA Modules:
  0.0 83.6 jit_solution(6268818082037633973)
XLA Ops:
  0.0 0.8 copy.26
  0.9 0.7 broadcast_in_dim.10
  1.6 11.7 %all-to-all-start = ((f32[16,32,128]{2,1,0:T(8,128)}), f32[16,32,128]{2,1,0:T(8,128)S(1)}, u32[]{:S(2)}, u32[]{:S(2)}) async-start(f32[16,32,128]{2,1,0:T(8,128)} %broadcast_in_dim.10), calls=%async_computation | async-start | bytes 524288 | tf_op jit(solution)/shard_map/all_to_all | solution.py:220
  13.4 1.0 %collective-permute-start.1 = (f32[4,8,64]{2,0,1:T(4,128)S(1)}, f32[4,8,64]{2,0,1:T(4,128)S(1)}, u32[]{:S(2)}, u32[]{:S(2)}) collective-permute-start(f32[4,8,64]{2,0,1:T(4,128)S(1)} %get-tuple-element.36), channel_id=1, source_target_pairs={{0,1},{1,0},{2,3},{3,2},{4,5},{5,4},{6,7},{7,6},{8,9},{9,8},{10,11... | collective-permute-start | bytes 24584 | tf_op jit(solution)/shard_map/ppermute | solution.py:187
  14.4 0.8 %collective-permute-done.1 = f32[4,8,64]{2,0,1:T(4,128)S(1)} collective-permute-done((f32[4,8,64]{2,0,1:T(4,128)S(1)}, f32[4,8,64]{2,0,1:T(4,128)S(1)}, u32[]{:S(2)}, u32[]{:S(2)}) %collective-permute-start.1) | collective-permute-done | bytes 8224 | tf_op jit(solution)/shard_map/ppermute | solution.py:187
  15.3 0.8 collective-permute-start.2
  16.1 2.7 %collective-permute-done.2 = f32[1,32,128]{2,1,0:T(8,128)S(1)} collective-permute-done((f32[1,32,128]{2,1,0:T(8,128)S(1)}, f32[1,32,128]{2,1,0:T(8,128)S(1)}, u32[]{:S(2)}, u32[]{:S(2)}) %collective-permute-start.2) | collective-permute-done | bytes 16416 | tf_op jit(solution)/shard_map/ppermute | solution.py:187
  18.8 1.3 %collective-permute-start.3 = (f32[2,32,128]{2,1,0:T(8,128)S(1)}, f32[2,32,128]{2,1,0:T(8,128)S(1)}, u32[]{:S(2)}, u32[]{:S(2)}) collective-permute-start(f32[2,32,128]{2,1,0:T(8,128)S(1)} %pad_maximum_fusion.2), channel_id=1, source_target_pairs={{0,64},{32,96},{64,0},{96,32},{128,192},{160,224},{192,128},{224,1... | collective-permute-start | bytes 98312 | tf_op jit(solution)/shard_map/ppermute | solution.py:187
  20.3 0.5 copy-done.10
  20.9 2.5 %all-to-all-done = f32[16,32,128]{2,1,0:T(8,128)S(1)} async-done(((f32[16,32,128]{2,1,0:T(8,128)}), f32[16,32,128]{2,1,0:T(8,128)S(1)}, u32[]{:S(2)}, u32[]{:S(2)}) %all-to-all-start) | async-done | bytes 262176 | tf_op jit(solution)/shard_map/all_to_all | solution.py:220
  23.5 3.7 %collective-permute-start = (f32[512,128]{1,0:T(8,128)S(1)}, f32[512,128]{1,0:T(8,128)S(1)}, u32[]{:S(2)}, u32[]{:S(2)}) collective-permute-start(f32[512,128]{1,0:T(8,128)S(1)} %bitcast.32), channel_id=1, source_target_pairs={{0,1},{1,0},{2,3},{3,2},{4,5},{5,4},{6,7},{7,6},{8,9},{9,8},{10,11... | collective-permute-start | bytes 786440 | tf_op jit(solution)/shard_map/ppermute | solution.py:187
  27.2 3.0 %collective-permute-start.4 = (f32[4,32,128]{2,1,0:T(8,128)S(1)}, f32[4,32,128]{2,1,0:T(8,128)S(1)}, u32[]{:S(2)}, u32[]{:S(2)}) collective-permute-start(f32[4,32,128]{2,1,0:T(8,128)S(1)} %pad_maximum_fusion.1), channel_id=1, source_target_pairs={{0,128},{32,160},{64,192},{96,224},{128,0},{160,32},{192,64},{224,... | collective-permute-start | bytes 196616 | tf_op jit(solution)/shard_map/ppermute | solution.py:187
  30.3 2.3 %collective-permute-done.4 = f32[4,32,128]{2,1,0:T(8,128)S(1)} collective-permute-done((f32[4,32,128]{2,1,0:T(8,128)S(1)}, f32[4,32,128]{2,1,0:T(8,128)S(1)}, u32[]{:S(2)}, u32[]{:S(2)}) %collective-permute-start.4) | collective-permute-done | bytes 65568 | tf_op jit(solution)/shard_map/ppermute | solution.py:187
  32.6 0.6 copy-done.2
  33.3 2.2 %shard_map.127 = (f32[512,128]{1,0:T(8,128)S(1)}, f32[256,128]{1,0:T(8,128)S(1)}, f32[128,256]{1,0:T(8,128)S(1)}) custom-call(s32[1]{0:T(128)} %bitcast.1.row_ref, f32[512,128]{1,0:T(8,128)S(1)} %bitcast.33, f32[512,128]{1,0:T(8,128)S(1)} %collective-permute-done.other_ref, f32[8,32,128]{2,1,0:T(8,128)S(1)} %pad_maximum_fusion.right_ref, ...), custom_call_target="tpu_custom_call" | custom-call | tf_op jit(solution)/shard_map/pallas_call | solution.py:175
  35.5 21.8 %all_to_all.30 = f32[128,4,128]{2,1,0:T(4,128)S(1)} all-to-all(f32[128,4,128]{2,1,0:T(4,128)S(1)} %bitcast.37), channel_id=1, replica_groups=mesh['row'=8,'col'=16,'seq'=2] {'row','col'}, dimensions={0} | all-to-all | bytes 524288 | tf_op jit(solution)/shard_map/all_to_all | solution.py:242
  57.3 4.3 %collective-permute-start.5 = (f32[512,128]{1,0:T(8,128)S(1)}, f32[512,128]{1,0:T(8,128)S(1)}, u32[]{:S(2)}, u32[]{:S(2)}) collective-permute-start(f32[512,128]{1,0:T(8,128)S(1)} %bitcast.34), channel_id=1, source_target_pairs={{0,1},{1,0},{2,3},{3,2},{4,5},{5,4},{6,7},{7,6},{8,9},{9,8},{10,11... | collective-permute-start | bytes 786440 | tf_op jit(solution)/shard_map/ppermute | solution.py:187
  61.6 1.2 %collective-permute-done.5.other_ref = f32[512,128]{1,0:T(8,128)S(1)} collective-permute-done((f32[512,128]{1,0:T(8,128)S(1)}, f32[512,128]{1,0:T(8,128)S(1)}, u32[]{:S(2)}, u32[]{:S(2)}) %collective-permute-start.5) | collective-permute-done | bytes 262176 | tf_op jit(solution)/shard_map/ppermute | solution.py:187
  62.8 1.4 %shard_map.128 = f32[256,128]{1,0:T(8,128)} custom-call(s32[1]{0:T(128)} %bitcast.core_ref, f32[512,128]{1,0:T(8,128)S(1)} %bitcast.35, f32[512,128]{1,0:T(8,128)S(1)} %collective-permute-done.5.other_ref), custom_call_target="tpu_custom_call" | custom-call | tf_op jit(solution)/shard_map/pallas_call | solution.py:175
  64.1 6.3 %all-to-all-start.2 = ((f32[128,2,128]{2,1,0:T(2,128)}), f32[128,2,128]{2,1,0:T(2,128)S(1)}, u32[]{:S(2)}, u32[]{:S(2)}) async-start(f32[128,2,128]{2,1,0:T(2,128)} %bitcast.16), calls=%async_computation.2 | async-start | bytes 262144 | tf_op jit(solution)/shard_map/all_to_all | solution.py:256
  70.6 0.7 copy-done.8
  71.4 10.5 %all-to-all-done.2 = f32[128,2,128]{2,1,0:T(2,128)S(1)} async-done(((f32[128,2,128]{2,1,0:T(2,128)}), f32[128,2,128]{2,1,0:T(2,128)S(1)}, u32[]{:S(2)}, u32[]{:S(2)}) %all-to-all-start.2) | async-done | bytes 131104 | tf_op jit(solution)/shard_map/all_to_all | solution.py:256
  81.9 0.7 copy-done.5
  82.6 1.0 %shard_map.129 = f32[256,128]{1,0:T(8,128)} custom-call(f32[256,128]{1,0:T(8,128)S(1)} %bitcast.36, f32[256,128]{1,0:T(8,128)S(1)} %get-tuple-element.33.updated_ref, f32[128,256]{1,0:T(8,128)S(1)} %get-tuple-element.34.gate_ref, f32[1,128]{1,0:T(1,128)S(1)} %bitcast.42, f32[1,128]{1,0:T(1,128)S(1)} %bitcast.43, f32[128,256]{1,0:T(8,128)S(1)} %fusion.1.weight_ref), custom_call_target="tpu_custom_call" | custom-call | tf_op jit(solution)/shard_map/pallas_call | solution.py:175
  (35 shorter events, 0.9 us)
Async XLA Ops:
  1.6 11.7 %copy-start.9 = (f32[64,16,4]{0,2,1:T(4,128)S(1)}, f32[64,16,4]{0,2,1:T(4,128)}, u32[]{:S(2)}) copy-start(f32[64,16,4]{0,2,1:T(4,128)} %param.19) | copy-start | bytes 49156
  1.6 18.5 %copy-start.7 = (f32[128,640]{1,0:T(8,128)S(1)}, f32[128,640]{1,0:T(8,128)}, u32[]{:S(2)}) copy-start(f32[128,640]{1,0:T(8,128)} %param.24) | copy-start | bytes 983044
  1.6 21.9 %all-to-all-start = ((f32[16,32,128]{2,1,0:T(8,128)}), f32[16,32,128]{2,1,0:T(8,128)S(1)}, u32[]{:S(2)}, u32[]{:S(2)}) async-start(f32[16,32,128]{2,1,0:T(8,128)} %broadcast_in_dim.10), calls=%async_computation | async-start | bytes 524288 | tf_op jit(solution)/shard_map/all_to_all | solution.py:220
  13.4 1.9 %collective-permute-start.1 = (f32[4,8,64]{2,0,1:T(4,128)S(1)}, f32[4,8,64]{2,0,1:T(4,128)S(1)}, u32[]{:S(2)}, u32[]{:S(2)}) collective-permute-start(f32[4,8,64]{2,0,1:T(4,128)S(1)} %get-tuple-element.36), channel_id=1, source_target_pairs={{0,1},{1,0},{2,3},{3,2},{4,5},{5,4},{6,7},{7,6},{8,9},{9,8},{10,11... | collective-permute-start | bytes 24584 | tf_op jit(solution)/shard_map/ppermute | solution.py:187
  15.3 3.5 %collective-permute-start.2 = (f32[1,32,128]{2,1,0:T(8,128)S(1)}, f32[1,32,128]{2,1,0:T(8,128)S(1)}, u32[]{:S(2)}, u32[]{:S(2)}) collective-permute-start(f32[1,32,128]{2,1,0:T(8,128)S(1)} %bitcast.44), channel_id=1, source_target_pairs={{0,32},{32,0},{64,96},{96,64},{128,160},{160,128},{192,224},{224,1... | collective-permute-start | bytes 49160 | tf_op jit(solution)/shard_map/ppermute | solution.py:187
  18.8 8.4 %collective-permute-start.3 = (f32[2,32,128]{2,1,0:T(8,128)S(1)}, f32[2,32,128]{2,1,0:T(8,128)S(1)}, u32[]{:S(2)}, u32[]{:S(2)}) collective-permute-start(f32[2,32,128]{2,1,0:T(8,128)S(1)} %pad_maximum_fusion.2), channel_id=1, source_target_pairs={{0,64},{32,96},{64,0},{96,32},{128,192},{160,224},{192,128},{224,1... | collective-permute-start | bytes 98312 | tf_op jit(solution)/shard_map/ppermute | solution.py:187
  20.1 0.7 copy-start.10
  23.5 9.1 %collective-permute-start = (f32[512,128]{1,0:T(8,128)S(1)}, f32[512,128]{1,0:T(8,128)S(1)}, u32[]{:S(2)}, u32[]{:S(2)}) collective-permute-start(f32[512,128]{1,0:T(8,128)S(1)} %bitcast.32), channel_id=1, source_target_pairs={{0,1},{1,0},{2,3},{3,2},{4,5},{5,4},{6,7},{7,6},{8,9},{9,8},{10,11... | collective-permute-start | bytes 786440 | tf_op jit(solution)/shard_map/ppermute | solution.py:187
  27.2 5.4 %copy-start = (f32[1024,128]{1,0:T(8,128)S(1)}, f32[1024,128]{1,0:T(8,128)}, u32[]{:S(2)}) copy-start(f32[1024,128]{1,0:T(8,128)} %mean_weight_ref.1) | copy-start | bytes 1572868
  27.2 5.3 %collective-permute-start.4 = (f32[4,32,128]{2,1,0:T(8,128)S(1)}, f32[4,32,128]{2,1,0:T(8,128)S(1)}, u32[]{:S(2)}, u32[]{:S(2)}) collective-permute-start(f32[4,32,128]{2,1,0:T(8,128)S(1)} %pad_maximum_fusion.1), channel_id=1, source_target_pairs={{0,128},{32,160},{64,192},{96,224},{128,0},{160,32},{192,64},{224,... | collective-permute-start | bytes 196616 | tf_op jit(solution)/shard_map/ppermute | solution.py:187
  30.3 2.3 %copy-start.1 = (f32[32,8,128]{2,1,0:T(8,128)S(1)}, f32[32,8,128]{2,1,0:T(8,128)}, u32[]{:S(2)}) copy-start(f32[32,8,128]{2,1,0:T(8,128)} %param.17) | copy-start | bytes 393220
  32.6 0.7 copy-start.2
  32.6 0.7 copy-start.3
  32.6 0.7 copy-start.4
  57.3 5.5 %collective-permute-start.5 = (f32[512,128]{1,0:T(8,128)S(1)}, f32[512,128]{1,0:T(8,128)S(1)}, u32[]{:S(2)}, u32[]{:S(2)}) collective-permute-start(f32[512,128]{1,0:T(8,128)S(1)} %bitcast.34), channel_id=1, source_target_pairs={{0,1},{1,0},{2,3},{3,2},{4,5},{5,4},{6,7},{7,6},{8,9},{9,8},{10,11... | collective-permute-start | bytes 786440 | tf_op jit(solution)/shard_map/ppermute | solution.py:187
  64.1 6.3 %copy-start.11 = (f32[128]{0:T(128)S(1)}, f32[128]{0:T(128)}, u32[]{:S(2)}) copy-start(f32[128]{0:T(128)} %param.29) | copy-start | bytes 1540
  64.1 17.8 %all-to-all-start.2 = ((f32[128,2,128]{2,1,0:T(2,128)}), f32[128,2,128]{2,1,0:T(2,128)S(1)}, u32[]{:S(2)}, u32[]{:S(2)}) async-start(f32[128,2,128]{2,1,0:T(2,128)} %bitcast.16), calls=%async_computation.2 | async-start | bytes 262144 | tf_op jit(solution)/shard_map/all_to_all | solution.py:256
  70.5 0.8 %copy-start.8 = (f32[128,128]{1,0:T(8,128)S(1)}, f32[128,128]{1,0:T(8,128)}, u32[]{:S(2)}) copy-start(f32[128,128]{1,0:T(8,128)} %param.28) | copy-start | bytes 196612
  81.9 0.7 copy-start.5
  81.9 0.7 copy-start.6

commit v2 on v1

v2 whole, which is shorter than its diff:
```python
import functools

import jax
import jax.numpy as jnp
from jax import lax
from jax.experimental import pallas as pl
from jax.experimental.pallas import tpu as pltpu
from jax.sharding import PartitionSpec as P

SEQUENCE_COUNT = 128
EPSILON = 1e-05
LANES = 128
VMEM_LIMIT = 32 * 1024 * 1024


def split(value):
    high = value.astype(jnp.bfloat16)
    return high, (value - high.astype(jnp.float32)).astype(jnp.bfloat16)


def product(left, right, transposed):
    dims = (((1,), (1 if transposed else 0,)), ((), ()))
    dot = functools.partial(
        lax.dot_general, dimension_numbers=dims, preferred_element_type=jnp.float32
    )
    return dot(left[0], right[0]) + (dot(left[0], right[1]) + dot(left[1], right[0]))


def swap_groups(blocks):
    lane = lax.broadcasted_iota(jnp.int32, blocks[0].shape, 1)
    wide, narrow = (lane & 64) == 0, (lane & 32) == 0

    def exchange(first, second, shift, mask):
        return (
            jnp.where(mask, first, pltpu.roll(second, shift, 1)),
            jnp.where(mask, pltpu.roll(first, LANES - shift, 1), second),
        )

    a, c = exchange(blocks[0], blocks[2], 64, wide)
    b, d = exchange(blocks[1], blocks[3], 64, wide)
    a, b = exchange(a, b, 32, narrow)
    c, d = exchange(c, d, 32, narrow)
    return a, b, c, d


def pack_kernel(core_ref, kept_ref, got_ref, vectors_ref, out_ref, vectors_out_ref):
    vectors_out_ref[...] = vectors_ref[...]
    first_core = core_ref[0] == 0

    def ordered(ref):
        left = [ref[pl.ds(p, 32, stride=2), :] for p in range(2)]
        right = [ref[pl.ds(q, 16, stride=4), :] for q in range(4)]
        return jnp.where(first_core, jnp.concatenate(left, axis=0), jnp.concatenate(right, axis=0))

    kept, got = ordered(kept_ref), ordered(got_ref)
    lower, upper = jnp.where(first_core, kept, got), jnp.where(first_core, got, kept)
    block = jnp.concatenate([lower, upper], axis=1)
    for n in range(16):
        out_ref[pl.ds(n * 64, 64), :] = block


def tile_kernel(
    place_ref,
    own_ref,
    other_ref,
    pair_ref,
    mean_weight_ref,
    weight_ref,
    vectors_ref,
    send_ref,
    updated_ref,
    gate_ref,
    right_scratch,
    high_scratch,
    low_scratch,
):
    core, odd = place_ref[0], place_ref[1]
    first_core = core == 0
    for row in range(8):
        for q in range(4):
            start = odd * 512 + row * 64 + q * 16 + core * 8
            rows = pl.ds(pl.multiple_of(start, 8), 8)
            right_scratch[pl.ds(row * 32 + q * 8, 8), :] = jnp.where(
                first_core, other_ref[rows, :], own_ref[rows, :]
            )
    right = split(
        jnp.concatenate([right_scratch[pl.ds(j, 32, stride=8), :] for j in range(8)], axis=0)
    )
    left = jnp.where(first_core, own_ref[...], other_ref[...])
    outer = product(split(left), right, True)
    for wide in range(2):
        for group in range(8):
            blocks = [
                outer[
                    (group * 4 + p) * 32 : (group * 4 + p + 1) * 32,
                    wide * LANES : (wide + 1) * LANES,
                ]
                for p in range(4)
            ]
            for j, block in enumerate(swap_groups(blocks)):
                rows = pl.ds((wide * 4 + j) * 32, 32)
                columns = pl.ds(group * LANES, LANES)
                high, low = split(block)
                high_scratch[rows, columns] = high
                low_scratch[rows, columns] = low
    summed = product(
        (high_scratch[...], low_scratch[...]), split(mean_weight_ref[...]), False
    )
    pair = jnp.concatenate([pair_ref[pl.ds(j, 32, stride=8), :] for j in range(8)], axis=0)
    updated = pair + (summed + vectors_ref[0:1]) * (1.0 / SEQUENCE_COUNT)
    updated_ref[...] = updated
    center = updated - jnp.mean(updated, axis=1, keepdims=True)
    spread = jnp.mean(center * center, axis=1, keepdims=True)
    normed = center * lax.rsqrt(spread + EPSILON) * vectors_ref[1:2] + vectors_ref[2:3]
    proj = product(split(normed), split(weight_ref[...]), False)
    blocks = [
        proj[:, n * LANES : (n + 1) * LANES] + vectors_ref[6 + n : 7 + n] for n in range(5)
    ]
    left_act = jnp.transpose(jax.nn.sigmoid(blocks[1]) * blocks[0])
    right_act = jnp.transpose(jax.nn.sigmoid(blocks[3]) * blocks[2])
    send_ref[pl.ds(0, 128, stride=4), :] = left_act[:, :LANES]
    send_ref[pl.ds(1, 128, stride=4), :] = left_act[:, LANES:]
    send_ref[pl.ds(2, 128, stride=4), :] = right_act[:, :LANES]
    send_ref[pl.ds(3, 128, stride=4), :] = right_act[:, LANES:]
    gate_ref[...] = jax.nn.sigmoid(blocks[4])


def triangle_kernel(core_ref, own_ref, other_ref, send_ref, left_scratch, right_scratch):
    first_core = core_ref[0] == 0

    def regroup(source, part, wide):
        return swap_groups([source(wide * 4 + r, part) for r in range(4)])

    def rows_of(ref):
        return lambda r, part: ref[pl.ds(r * 64 + part, 16, stride=4), :]

    own, other = rows_of(own_ref), rows_of(other_ref)

    def lower(r, part):
        return jnp.where(first_core, own(r, part), other(r, part))

    def upper(r, part):
        return jnp.where(first_core, other(r, part), own(r, part))

    for wide in range(2):
        for part in range(2):
            for core, source in enumerate((lower, upper)):
                for g, block in enumerate(regroup(source, part, wide)):
                    place = core * 8 + part * 4 + g
                    left_scratch[wide, pl.ds(place, 16, stride=16), :] = block
            for g, block in enumerate(regroup(own, part + 2, wide)):
                right_scratch[wide, pl.ds((part * 4 + g) * 16, 16), :] = block
    left = split(jnp.concatenate([left_scratch[0], left_scratch[1]], axis=1))
    right = split(jnp.concatenate([right_scratch[0], right_scratch[1]], axis=1))
    mixed = product(right, left, True)
    for wide in range(2):
        for part in range(2):
            blocks = [
                mixed[
                    (part * 4 + g) * 16 : (part * 4 + g + 1) * 16,
                    wide * LANES : (wide + 1) * LANES,
                ]
                for g in range(4)
            ]
            for r, block in enumerate(swap_groups(blocks)):
                send_ref[pl.ds((wide * 4 + r) * 32 + part, 16, stride=2), :] = block


def output_kernel(mixed_ref, updated_ref, gate_ref, weight_ref, vectors_ref, out_ref):
    mixed = jnp.concatenate(
        [mixed_ref[pl.ds(0, 128, stride=2), :], mixed_ref[pl.ds(1, 128, stride=2), :]], axis=1
    )
    center = mixed - jnp.mean(mixed, axis=0, keepdims=True)
    spread = jnp.mean(center * center, axis=0, keepdims=True)
    normed = jnp.transpose(center * lax.rsqrt(spread + EPSILON))
    normed = normed * vectors_ref[3:4] + vectors_ref[4:5]
    result = product(split(normed), split(weight_ref[...]), False) + vectors_ref[5:6]
    out = updated_ref[...] + gate_ref[...] * result
    for j in range(8):
        out_ref[pl.ds(j, 32, stride=8), :] = out[j * 32 : (j + 1) * 32]


def call(kernel, outputs, scratch, scalars, *blocks):
    specs = [pl.BlockSpec(memory_space=pltpu.SMEM)] * len(scalars)
    specs += [pl.BlockSpec(memory_space=pltpu.VMEM)] * len(blocks)
    return pl.pallas_call(
        kernel,
        out_shape=[jax.ShapeDtypeStruct(shape, jnp.float32) for shape in outputs],
        in_specs=specs,
        out_specs=[pl.BlockSpec(memory_space=pltpu.VMEM)] * len(outputs),
        scratch_shapes=scratch,
        compiler_params=pltpu.CompilerParams(vmem_limit_bytes=VMEM_LIMIT),
    )(*scalars, *blocks)


def exchange(value, axis, distance):
    count = lax.axis_size(axis)
    return lax.ppermute(value, axis, [(n, n ^ distance) for n in range(count)])


def gather_groups(rows, columns):
    place = lambda row, column, core: (row * columns + column) * 2 + core
    first = [[place(row, column, 0) for column in range(columns)] for row in range(rows)]
    second = [
        [place(row, column + n, 1) for n in range(2) for row in range(rows)]
        for column in range(0, columns, 2)
    ]
    return first + second


def per_device(
    pair,
    alignment_left,
    alignment_right,
    outer_mean_weight,
    outer_mean_bias,
    input_norm_gain,
    input_norm_bias,
    input_weight_matrix,
    input_bias_vector,
    output_norm_gain,
    output_norm_bias,
    output_weight_matrix,
    output_bias_vector,
):
    core = lax.axis_index("seq")
    place = jnp.stack([core, lax.axis_index("col") % 2])
    core_array = core.reshape(1)
    left = alignment_left.transpose(1, 2, 0).reshape(64, 64)
    right = alignment_right.transpose(1, 2, 0).reshape(64, 64)
    kept = jnp.where(core == 0, left, right)
    got = exchange(jnp.where(core == 0, right, left), "seq", 1)
    vectors = [
        outer_mean_bias,
        input_norm_gain,
        input_norm_bias,
        output_norm_gain,
        output_norm_bias,
        output_bias_vector,
        input_bias_vector,
    ]
    vectors = jnp.concatenate([vector.reshape(-1, LANES) for vector in vectors], axis=0)
    blocks, vectors = call(
        pack_kernel,
        [(1024, LANES), vectors.shape],
        [],
        [core_array],
        kept,
        got,
        vectors,
    )
    own = lax.all_to_all(
        blocks,
        ("row", "col", "seq"),
        0,
        0,
        tiled=True,
        axis_index_groups=gather_groups(lax.axis_size("row"), lax.axis_size("col")),
    )
    send, updated, gate = call(
        tile_kernel,
        [(512, LANES), (256, LANES), (256, LANES)],
        [
            pltpu.VMEM((256, LANES), jnp.float32),
            pltpu.VMEM((256, 1024), jnp.bfloat16),
            pltpu.VMEM((256, 1024), jnp.bfloat16),
        ],
        [place],
        own,
        exchange(own, "seq", 1),
        pair.reshape(256, LANES),
        outer_mean_weight,
        input_weight_matrix,
        vectors,
    )
    own = lax.all_to_all(send, ("row", "col"), 0, 0, tiled=True)
    (back,) = call(
        triangle_kernel,
        [(256, LANES)],
        [
            pltpu.VMEM((2, 256, LANES), jnp.float32),
            pltpu.VMEM((2, 128, LANES), jnp.float32),
        ],
        [core_array],
        own,
        exchange(own, "seq", 1),
    )
    mixed = lax.all_to_all(back, ("row", "col"), 0, 0, tiled=True)
    (out,) = call(
        output_kernel,
        [(256, LANES)],
        [],
        [],
        mixed,
        updated,
        gate,
        output_weight_matrix,
        vectors,
    )
    return out.reshape(pair.shape)


def solution(mesh):
    return jax.shard_map(
        per_device,
        mesh=mesh,
        in_specs=(
            P("row", ("col", "seq"), None),
            P("seq", "row", "col"),
            P("seq", "col", "row"),
            P(),
            P(),
            P(),
            P(),
            P(),
            P(),
            P(),
            P(),
            P(),
            P(),
        ),
        out_specs=P("row", ("col", "seq"), None),
        check_vma=False,
    )
```

time: 84.1 us -> 78.1 us (0.929)
  blocking collectives: 21.8 us -> 51.9 us
  waiting for transfers between devices: 20 us -> 2.63 us
  starting transfers between devices: 32.2 us -> 16.4 us
  local copies, waits for them, and re-layouts: 4.69 us -> 0.85 us
    all_to_all x0 -> x2, blocking collectives: none -> 29.4 us  [the longest x1 17.1 us: per_device(): mixed = lax.all_to_all(back, ('row', 'col'), 0, 0, tiled=True)]
    all_to_all x2 -> x0, starting transfers between devices: 18 us -> none  [the longest x1 11.7 us: per_device(): own = lax.all_to_all(left, 'col', 0, 0, tiled=True)]
    all_to_all x2 -> x0, waiting for transfers between devices: 13.1 us -> none  [the longest x1 10.5 us: per_device(): mixed = lax.all_to_all(back, ('row', 'col'), 0, 0, tiled=True)]
    ppermute x6 -> x3, waiting for transfers between devices: 6.93 us -> 2.63 us  [exchange(): return lax.ppermute(value, axis, [(n, n ^ distance) for n in range(count)])]
    ppermute x6 -> x3, starting transfers between devices: 14.2 us -> 16.4 us  [exchange(): return lax.ppermute(value, axis, [(n, n ^ distance) for n in range(count)])]
    unnamed x26 -> x22, local copies, waits for them, and re-layouts: 2.82 us -> 0.74 us
    pallas_call x3 -> x4, Pallas kernels: 4.62 us -> 5.11 us  [call(): pl.pallas_call(kernel, out_shape=[jax.ShapeDtypeStruct(shape, jnp.float32...]
  transfers between devices with their start and end apart: 8 -> 3, of which waited for: 6 -> 2; matrix products, arithmetic and copies ran while one was open for 1% -> 0% of each run, Pallas kernels for 0% -> 0%
where the time goes in v2:
time: 78.1 us; the launch traced here: 77.8 us
  blocking collectives  51.9 us (66%)
  starting transfers between devices  16.4 us (21%)
  Pallas kernels  5.11 us (7%)
  waiting for transfers between devices  2.63 us (3%)
  other arithmetic  0.86 us (1%)
  local copies, waits for them, and re-layouts  0.85 us (1%)
    all_to_all x1, blocking collectives, per_device(): own = lax.all_to_all(send, ('row', 'col'), 0, 0, tiled=True)  22.5 us
    all_to_all x1, blocking collectives, per_device(): mixed = lax.all_to_all(back, ('row', 'col'), 0, 0, tiled=True)  17.1 us
    ppermute x3, starting transfers between devices, exchange(): return lax.ppermute(value, axis, [(n, n ^ distance) for n in range(count)])  16.4 us
    all_to_all x1, blocking collectives, per_device(): lax.all_to_all(blocks, ('row', 'col', 'seq'), 0, 0, tiled=True, axis_inde...  12.3 us
    pallas_call x4, Pallas kernels, call(): pl.pallas_call(kernel, out_shape=[jax.ShapeDtypeStruct(shape, jnp.float32...  5.11 us
    ppermute x3, waiting for transfers between devices, exchange(): return lax.ppermute(value, axis, [(n, n ^ distance) for n in range(count)])  2.63 us
  transfers between devices with their start and end apart: 3, of which 2 were waited for; matrix products, arithmetic and copies ran while one was open for 0% of the time, Pallas kernels for 0%

profile of v2, /device:TPU:1, one launch (start us, length us, event | category | flops | bytes accessed | tf_op | source)
XLA Modules:
  0.0 77.8 jit_solution(3663296922087950365)
XLA Ops:
  0.0 0.8 %broadcast_select_fusion = (f32[64,64]{1,0:T(8,128)S(1)}, f32[64,64]{1,0:T(8,128)S(1)}) fusion(f32[64,64]{1,0:T(8,128)} %bitcast.32, f32[64,64]{1,0:T(8,128)} %bitcast.33, pred[]{:T(512)S(6)} %eq.6), kind=kLoop, calls=%fused_computation | loop fusion | flops 8192 | bytes 65537 | tf_op jit(solution)/shard_map/jit(_where)/select_n | solution.py:232
  0.8 3.2 %collective-permute-start = (f32[64,64]{1,0:T(8,128)S(1)}, f32[64,64]{1,0:T(8,128)S(1)}, u32[]{:S(2)}, u32[]{:S(2)}) collective-permute-start(f32[64,64]{1,0:T(8,128)S(1)} %get-tuple-element.15), channel_id=1, source_target_pairs={{0,1},{1,0},{2,3},{3,2},{4,5},{5,4},{6,7},{7,6},{8,9},{9,8},{10,11... | collective-permute-start | bytes 49160 | tf_op jit(solution)/shard_map/ppermute | solution.py:198
  4.0 0.0 copy-start.6
  4.1 0.0 copy-start.7
  4.1 0.6 copy-done.4
  4.7 0.0 copy-done.10
  4.7 0.0 copy-done.5
  4.7 0.0 copy-done.6
  4.8 0.0 copy-done.7
  4.8 0.1 concatenate.3.vectors_ref
  4.9 0.1 shard_map.127
  5.0 0.0 copy-start.1
  5.0 0.0 copy-start.2
  5.1 12.3 %all_to_all.33 = f32[16,64,128]{2,1,0:T(8,128)S(1)} all-to-all(f32[16,64,128]{2,1,0:T(8,128)S(1)} %bitcast.27), channel_id=1, replica_groups={{0,2,4,6,8,10,12,14,16,18,20,22,24,26,28,30},{32,34,36,38,40,42,44,46,4..., dimensions={0} | all-to-all | bytes 1048576 | tf_op jit(solution)/shard_map/all_to_all | solution.py:252
  17.3 10.6 %collective-permute-start.1 = (f32[1024,128]{1,0:T(8,128)S(1)}, f32[1024,128]{1,0:T(8,128)S(1)}, u32[]{:S(2)}, u32[]{:S(2)}) collective-permute-start(f32[1024,128]{1,0:T(8,128)S(1)} %bitcast.23), channel_id=1, source_target_pairs={{0,1},{1,0},{2,3},{3,2},{4,5},{5,4},{6,7},{7,6},{8,9},{9,8},{10,11... | collective-permute-start | bytes 1572872 | tf_op jit(solution)/shard_map/ppermute | solution.py:198
  27.9 0.1 pad_add_fusion.place_ref
  28.0 1.5 %collective-permute-done.1.other_ref = f32[1024,128]{1,0:T(8,128)S(1)} collective-permute-done((f32[1024,128]{1,0:T(8,128)S(1)}, f32[1024,128]{1,0:T(8,128)S(1)}, u32[]{:S(2)}, u32[]{:S(2)}) %collective-permute-start.1) | collective-permute-done | bytes 524320 | tf_op jit(solution)/shard_map/ppermute | solution.py:198
  29.4 3.3 %shard_map.128 = (f32[512,128]{1,0:T(8,128)S(1)}, f32[256,128]{1,0:T(8,128)S(1)}, f32[256,128]{1,0:T(8,128)S(1)}) custom-call(s32[2]{0:T(128)S(1)} %pad_add_fusion.place_ref, f32[1024,128]{1,0:T(8,128)S(1)} %bitcast.24, f32[1024,128]{1,0:T(8,128)S(1)} %collective-permute-done.1.other_ref, f32[256,128]{1,0:T(8,128)S(1)} %bitcast.31, f32[1024,128]{1,0:T(8,128)S(1)} %copy-done, ...), custom_call_target="tpu_custom_call" | custom-call | tf_op jit(solution)/shard_map/pallas_call | solution.py:186
  32.7 22.5 %all_to_all.34 = f32[128,4,128]{2,1,0:T(4,128)S(1)} all-to-all(f32[128,4,128]{2,1,0:T(4,128)S(1)} %bitcast.30), channel_id=1, replica_groups=mesh['row'=8,'col'=16,'seq'=2] {'row','col'}, dimensions={0} | all-to-all | bytes 524288 | tf_op jit(solution)/shard_map/all_to_all | solution.py:276
  55.2 2.5 %collective-permute-start.2 = (f32[512,128]{1,0:T(8,128)S(1)}, f32[512,128]{1,0:T(8,128)S(1)}, u32[]{:S(2)}, u32[]{:S(2)}) collective-permute-start(f32[512,128]{1,0:T(8,128)S(1)} %bitcast.25), channel_id=1, source_target_pairs={{0,1},{1,0},{2,3},{3,2},{4,5},{5,4},{6,7},{7,6},{8,9},{9,8},{10,11... | collective-permute-start | bytes 786440 | tf_op jit(solution)/shard_map/ppermute | solution.py:198
  57.8 1.2 %collective-permute-done.2.other_ref = f32[512,128]{1,0:T(8,128)S(1)} collective-permute-done((f32[512,128]{1,0:T(8,128)S(1)}, f32[512,128]{1,0:T(8,128)S(1)}, u32[]{:S(2)}, u32[]{:S(2)}) %collective-permute-start.2) | collective-permute-done | bytes 262176 | tf_op jit(solution)/shard_map/ppermute | solution.py:198
  58.9 0.7 shard_map.129
  59.7 17.1 %all_to_all.35 = f32[128,2,128]{2,1,0:T(2,128)S(1)} all-to-all(f32[128,2,128]{2,1,0:T(2,128)S(1)} %bitcast.29), channel_id=1, replica_groups=mesh['row'=8,'col'=16,'seq'=2] {'row','col'}, dimensions={0} | all-to-all | bytes 262144 | tf_op jit(solution)/shard_map/all_to_all | solution.py:288
  76.8 1.0 %shard_map.130 = f32[256,128]{1,0:T(8,128)} custom-call(f32[256,128]{1,0:T(8,128)S(1)} %bitcast.28, f32[256,128]{1,0:T(8,128)S(1)} %get-tuple-element.13.updated_ref, f32[256,128]{1,0:T(8,128)S(1)} %get-tuple-element.14.gate_ref, f32[128,128]{1,0:T(8,128)S(1)} %copy-done.3, f32[11,128]{1,0:T(8,128)S(1)} %get-tuple-element.11.vectors_ref), custom_call_target="tpu_custom_call" | custom-call | tf_op jit(solution)/shard_map/pallas_call | solution.py:186
  (14 shorter events, 0.0 us)
Async XLA Ops:
  0.8 4.1 %collective-permute-start = (f32[64,64]{1,0:T(8,128)S(1)}, f32[64,64]{1,0:T(8,128)S(1)}, u32[]{:S(2)}, u32[]{:S(2)}) collective-permute-start(f32[64,64]{1,0:T(8,128)S(1)} %get-tuple-element.15), channel_id=1, source_target_pairs={{0,1},{1,0},{2,3},{3,2},{4,5},{5,4},{6,7},{7,6},{8,9},{9,8},{10,11... | collective-permute-start | bytes 49160 | tf_op jit(solution)/shard_map/ppermute | solution.py:198
  4.0 0.7 copy-start.4
  4.0 0.7 copy-start.8
  4.0 0.7 copy-start.9
  4.0 0.7 copy-start.10
  4.0 0.7 copy-start.5
  4.0 0.7 copy-start.6
  4.1 0.7 copy-start.7
  5.0 24.4 %copy-start = (f32[1024,128]{1,0:T(8,128)S(1)}, f32[1024,128]{1,0:T(8,128)}, u32[]{:S(2)}) copy-start(f32[1024,128]{1,0:T(8,128)} %mean_weight_ref.1) | copy-start | bytes 1572868
  5.0 24.4 %copy-start.1 = (f32[128,640]{1,0:T(8,128)S(1)}, f32[128,640]{1,0:T(8,128)}, u32[]{:S(2)}) copy-start(f32[128,640]{1,0:T(8,128)} %weight_ref.2) | copy-start | bytes 983044
  5.0 24.4 %copy-start.2 = (f32[32,8,128]{2,1,0:T(8,128)S(1)}, f32[32,8,128]{2,1,0:T(8,128)}, u32[]{:S(2)}) copy-start(f32[32,8,128]{2,1,0:T(8,128)} %param.13) | copy-start | bytes 393220
  17.3 12.1 %collective-permute-start.1 = (f32[1024,128]{1,0:T(8,128)S(1)}, f32[1024,128]{1,0:T(8,128)S(1)}, u32[]{:S(2)}, u32[]{:S(2)}) collective-permute-start(f32[1024,128]{1,0:T(8,128)S(1)} %bitcast.23), channel_id=1, source_target_pairs={{0,1},{1,0},{2,3},{3,2},{4,5},{5,4},{6,7},{7,6},{8,9},{9,8},{10,11... | collective-permute-start | bytes 1572872 | tf_op jit(solution)/shard_map/ppermute | solution.py:198
  55.2 3.7 %collective-permute-start.2 = (f32[512,128]{1,0:T(8,128)S(1)}, f32[512,128]{1,0:T(8,128)S(1)}, u32[]{:S(2)}, u32[]{:S(2)}) collective-permute-start(f32[512,128]{1,0:T(8,128)S(1)} %bitcast.25), channel_id=1, source_target_pairs={{0,1},{1,0},{2,3},{3,2},{4,5},{5,4},{6,7},{7,6},{8,9},{9,8},{10,11... | collective-permute-start | bytes 786440 | tf_op jit(solution)/shard_map/ppermute | solution.py:198
  59.7 17.1 %copy-start.3 = (f32[128,128]{1,0:T(8,128)S(1)}, f32[128,128]{1,0:T(8,128)}, u32[]{:S(2)}) copy-start(f32[128,128]{1,0:T(8,128)} %weight_ref.3) | copy-start | bytes 196612

commit v3 on v2

--- a/solution.py
+++ b/solution.py
@@ -11,6 +11,7 @@
 EPSILON = 1e-05
 LANES = 128
 VMEM_LIMIT = 32 * 1024 * 1024
+FAR_ROW, FAR_COLUMN = 4, 10
 
 
 def split(value):
@@ -80,7 +81,7 @@
         for q in range(4):
             start = odd * 512 + row * 64 + q * 16 + core * 8
             rows = pl.ds(pl.multiple_of(start, 8), 8)
-            right_scratch[pl.ds(row * 32 + q * 8, 8), :] = jnp.where(
+            right_scratch[pl.ds((row ^ FAR_ROW) * 32 + q * 8, 8), :] = jnp.where(
                 first_core, other_ref[rows, :], own_ref[rows, :]
             )
     right = split(
@@ -99,7 +100,7 @@
             ]
             for j, block in enumerate(swap_groups(blocks)):
                 rows = pl.ds((wide * 4 + j) * 32, 32)
-                columns = pl.ds(group * LANES, LANES)
+                columns = pl.ds((group ^ (FAR_COLUMN // 2)) * LANES, LANES)
                 high, low = split(block)
                 high_scratch[rows, columns] = high
                 low_scratch[rows, columns] = low
@@ -163,7 +164,8 @@
                 for g in range(4)
             ]
             for r, block in enumerate(swap_groups(blocks)):
-                send_ref[pl.ds((wide * 4 + r) * 32 + part, 16, stride=2), :] = block
+                place = (wide * 4 + r) ^ (FAR_COLUMN // 2) ^ FAR_ROW
+                send_ref[pl.ds(place * 32 + part, 16, stride=2), :] = block
 
 
 def output_kernel(mixed_ref, updated_ref, gate_ref, weight_ref, vectors_ref, out_ref):
@@ -198,11 +200,22 @@
     return lax.ppermute(value, axis, [(n, n ^ distance) for n in range(count)])
 
 
+def far_first(rows, columns):
+    return [(row ^ FAR_ROW, column ^ FAR_COLUMN) for row in range(rows) for column in range(columns)]
+
+
+def exchange_groups(rows, columns):
+    places = far_first(rows, columns)
+    return [[(row * columns + column) * 2 + core for row, column in places] for core in range(2)]
+
+
 def gather_groups(rows, columns):
     place = lambda row, column, core: (row * columns + column) * 2 + core
-    first = [[place(row, column, 0) for column in range(columns)] for row in range(rows)]
+    first = [
+        [place(row, column ^ FAR_COLUMN, 0) for column in range(columns)] for row in range(rows)
+    ]
     second = [
-        [place(row, column + n, 1) for n in range(2) for row in range(rows)]
+        [place(row ^ FAR_ROW, column + n, 1) for n in range(2) for row in range(rows)]
         for column in range(0, columns, 2)
     ]
     return first + second
@@ -223,6 +236,13 @@
     output_weight_matrix,
     output_bias_vector,
 ):
+    rows, columns = lax.axis_size("row"), lax.axis_size("col")
+
+    def spread(value, groups):
+        return lax.all_to_all(
+            value, ("row", "col", "seq"), 0, 0, tiled=True, axis_index_groups=groups
+        )
+
     core = lax.axis_index("seq")
     place = jnp.stack([core, lax.axis_index("col") % 2])
     core_array = core.reshape(1)
@@ -249,14 +269,7 @@
         got,
         vectors,
     )
-    own = lax.all_to_all(
-        blocks,
-        ("row", "col", "seq"),
-        0,
-        0,
-        tiled=True,
-        axis_index_groups=gather_groups(lax.axis_size("row"), lax.axis_size("col")),
-    )
+    own = spread(blocks, gather_groups(rows, columns))
     send, updated, gate = call(
         tile_kernel,
         [(512, LANES), (256, LANES), (256, LANES)],
@@ -273,7 +286,7 @@
         input_weight_matrix,
         vectors,
     )
-    own = lax.all_to_all(send, ("row", "col"), 0, 0, tiled=True)
+    own = spread(send, exchange_groups(rows, columns))
     (back,) = call(
         triangle_kernel,
         [(256, LANES)],
@@ -285,7 +298,7 @@
         own,
         exchange(own, "seq", 1),
     )
-    mixed = lax.all_to_all(back, ("row", "col"), 0, 0, tiled=True)
+    mixed = spread(back, exchange_groups(rows, columns))
     (out,) = call(
         output_kernel,
         [(256, LANES)],

time: 78.1 us -> 73.1 us (0.936)
  starting transfers between devices: 16.4 us -> 12.5 us
  blocking collectives: 51.9 us -> 50.8 us
    ppermute x3, starting transfers between devices: 16.4 us -> 12.5 us  [exchange(): return lax.ppermute(value, axis, [(n, n ^ distance) for n in range(count)])]
    all_to_all x3, blocking collectives: 51.9 us -> 50.8 us  [spread(): lax.all_to_all(value, ('row', 'col', 'seq'), 0, 0, tiled=True, axis_index...]
where the time goes in v3:
time: 73.1 us; the launch traced here: 72.8 us
  blocking collectives  50.8 us (69%)
  starting transfers between devices  12.5 us (17%)
  Pallas kernels  5.14 us (7%)
  waiting for transfers between devices  2.63 us (4%)
  other arithmetic  0.86 us (1%)
  local copies, waits for them, and re-layouts  0.85 us (1%)
    all_to_all x3, blocking collectives, spread(): lax.all_to_all(value, ('row', 'col', 'seq'), 0, 0, tiled=True, axis_index...  50.8 us
    ppermute x3, starting transfers between devices, exchange(): return lax.ppermute(value, axis, [(n, n ^ distance) for n in range(count)])  12.5 us
    pallas_call x4, Pallas kernels, call(): pl.pallas_call(kernel, out_shape=[jax.ShapeDtypeStruct(shape, jnp.float32...  5.14 us
    ppermute x3, waiting for transfers between devices, exchange(): return lax.ppermute(value, axis, [(n, n ^ distance) for n in range(count)])  2.63 us
  transfers between devices with their start and end apart: 3, of which 2 were waited for; matrix products, arithmetic and copies ran while one was open for 0% of the time, Pallas kernels for 0%

profile of v3, /device:TPU:1, one launch (start us, length us, event | category | flops | bytes accessed | tf_op | source)
XLA Modules:
  0.0 72.8 jit_solution(17840654217250680691)
XLA Ops:
  0.0 0.8 %broadcast_select_fusion = (f32[64,64]{1,0:T(8,128)S(1)}, f32[64,64]{1,0:T(8,128)S(1)}) fusion(f32[64,64]{1,0:T(8,128)} %bitcast.32, f32[64,64]{1,0:T(8,128)} %bitcast.33, pred[]{:T(512)S(6)} %eq.6), kind=kLoop, calls=%fused_computation | loop fusion | flops 8192 | bytes 65537 | tf_op jit(solution)/shard_map/jit(_where)/select_n | solution.py:252
  0.8 3.2 %collective-permute-start = (f32[64,64]{1,0:T(8,128)S(1)}, f32[64,64]{1,0:T(8,128)S(1)}, u32[]{:S(2)}, u32[]{:S(2)}) collective-permute-start(f32[64,64]{1,0:T(8,128)S(1)} %get-tuple-element.15), channel_id=1, source_target_pairs={{0,1},{1,0},{2,3},{3,2},{4,5},{5,4},{6,7},{7,6},{8,9},{9,8},{10,11... | collective-permute-start | bytes 49160 | tf_op jit(solution)/shard_map/ppermute | solution.py:200
  4.0 0.0 copy-start.5
  4.0 0.0 copy-start.6
  4.1 0.0 copy-start.7
  4.1 0.6 copy-done.4
  4.7 0.0 copy-done.10
  4.7 0.0 copy-done.5
  4.7 0.0 copy-done.6
  4.8 0.0 copy-done.7
  4.8 0.1 concatenate.3.vectors_ref
  4.9 0.1 shard_map.127
  5.0 0.0 copy-start
  5.1 11.2 %all_to_all.33 = f32[16,64,128]{2,1,0:T(8,128)S(1)} all-to-all(f32[16,64,128]{2,1,0:T(8,128)S(1)} %bitcast.27), channel_id=1, replica_groups={{20,22,16,18,28,30,24,26,4,6,0,2,12,14,8,10},{52,54,48,50,60,62,56,58,3..., dimensions={0} | all-to-all | bytes 1048576 | tf_op jit(solution)/shard_map/all_to_all | solution.py:242
  16.2 8.5 %collective-permute-start.1 = (f32[1024,128]{1,0:T(8,128)S(1)}, f32[1024,128]{1,0:T(8,128)S(1)}, u32[]{:S(2)}, u32[]{:S(2)}) collective-permute-start(f32[1024,128]{1,0:T(8,128)S(1)} %bitcast.23), channel_id=1, source_target_pairs={{0,1},{1,0},{2,3},{3,2},{4,5},{5,4},{6,7},{7,6},{8,9},{9,8},{10,11... | collective-permute-start | bytes 1572872 | tf_op jit(solution)/shard_map/ppermute | solution.py:200
  24.7 0.1 pad_add_fusion.place_ref
  24.8 1.5 %collective-permute-done.1.other_ref = f32[1024,128]{1,0:T(8,128)S(1)} collective-permute-done((f32[1024,128]{1,0:T(8,128)S(1)}, f32[1024,128]{1,0:T(8,128)S(1)}, u32[]{:S(2)}, u32[]{:S(2)}) %collective-permute-start.1) | collective-permute-done | bytes 524320 | tf_op jit(solution)/shard_map/ppermute | solution.py:200
  26.3 3.3 %shard_map.128 = (f32[512,128]{1,0:T(8,128)S(1)}, f32[256,128]{1,0:T(8,128)S(1)}, f32[256,128]{1,0:T(8,128)S(1)}) custom-call(s32[2]{0:T(128)S(1)} %pad_add_fusion.place_ref, f32[1024,128]{1,0:T(8,128)S(1)} %bitcast.24, f32[1024,128]{1,0:T(8,128)S(1)} %collective-permute-done.1.other_ref, f32[256,128]{1,0:T(8,128)S(1)} %bitcast.31, f32[1024,128]{1,0:T(8,128)S(1)} %copy-done, ...), custom_call_target="tpu_custom_call" | custom-call | tf_op jit(solution)/shard_map/pallas_call | solution.py:188
  29.6 21.6 %all_to_all.34 = f32[128,4,128]{2,1,0:T(4,128)S(1)} all-to-all(f32[128,4,128]{2,1,0:T(4,128)S(1)} %bitcast.30), channel_id=1, replica_groups={{148,150,144,146,156,158,152,154,132,134,128,130,140,142,136,138,180,18..., dimensions={0} | all-to-all | bytes 524288 | tf_op jit(solution)/shard_map/all_to_all | solution.py:242
  51.2 0.7 %collective-permute-start.2 = (f32[512,128]{1,0:T(8,128)S(1)}, f32[512,128]{1,0:T(8,128)S(1)}, u32[]{:S(2)}, u32[]{:S(2)}) collective-permute-start(f32[512,128]{1,0:T(8,128)S(1)} %bitcast.25), channel_id=1, source_target_pairs={{0,1},{1,0},{2,3},{3,2},{4,5},{5,4},{6,7},{7,6},{8,9},{9,8},{10,11... | collective-permute-start | bytes 786440 | tf_op jit(solution)/shard_map/ppermute | solution.py:200
  51.9 1.2 %collective-permute-done.2.other_ref = f32[512,128]{1,0:T(8,128)S(1)} collective-permute-done((f32[512,128]{1,0:T(8,128)S(1)}, f32[512,128]{1,0:T(8,128)S(1)}, u32[]{:S(2)}, u32[]{:S(2)}) %collective-permute-start.2) | collective-permute-done | bytes 262176 | tf_op jit(solution)/shard_map/ppermute | solution.py:200
  53.1 0.7 shard_map.129
  53.8 18.0 %all_to_all.35 = f32[128,2,128]{2,1,0:T(2,128)S(1)} all-to-all(f32[128,2,128]{2,1,0:T(2,128)S(1)} %bitcast.29), channel_id=1, replica_groups={{148,150,144,146,156,158,152,154,132,134,128,130,140,142,136,138,180,18..., dimensions={0} | all-to-all | bytes 262144 | tf_op jit(solution)/shard_map/all_to_all | solution.py:242
  71.8 1.0 %shard_map.130 = f32[256,128]{1,0:T(8,128)} custom-call(f32[256,128]{1,0:T(8,128)S(1)} %bitcast.28, f32[256,128]{1,0:T(8,128)S(1)} %get-tuple-element.13.updated_ref, f32[256,128]{1,0:T(8,128)S(1)} %get-tuple-element.14.gate_ref, f32[128,128]{1,0:T(8,128)S(1)} %copy-done.3, f32[11,128]{1,0:T(8,128)S(1)} %get-tuple-element.11.vectors_ref), custom_call_target="tpu_custom_call" | custom-call | tf_op jit(solution)/shard_map/pallas_call | solution.py:188
  (14 shorter events, 0.0 us)
Async XLA Ops:
  0.8 4.1 %collective-permute-start = (f32[64,64]{1,0:T(8,128)S(1)}, f32[64,64]{1,0:T(8,128)S(1)}, u32[]{:S(2)}, u32[]{:S(2)}) collective-permute-start(f32[64,64]{1,0:T(8,128)S(1)} %get-tuple-element.15), channel_id=1, source_target_pairs={{0,1},{1,0},{2,3},{3,2},{4,5},{5,4},{6,7},{7,6},{8,9},{9,8},{10,11... | collective-permute-start | bytes 49160 | tf_op jit(solution)/shard_map/ppermute | solution.py:200
  4.0 0.7 copy-start.4
  4.0 0.7 copy-start.8
  4.0 0.7 copy-start.9
  4.0 0.7 copy-start.10
  4.0 0.7 copy-start.5
  4.0 0.7 copy-start.6
  4.1 0.7 copy-start.7
  5.0 21.2 %copy-start = (f32[1024,128]{1,0:T(8,128)S(1)}, f32[1024,128]{1,0:T(8,128)}, u32[]{:S(2)}) copy-start(f32[1024,128]{1,0:T(8,128)} %mean_weight_ref.1) | copy-start | bytes 1572868
  5.0 21.2 %copy-start.1 = (f32[128,640]{1,0:T(8,128)S(1)}, f32[128,640]{1,0:T(8,128)}, u32[]{:S(2)}) copy-start(f32[128,640]{1,0:T(8,128)} %weight_ref.2) | copy-start | bytes 983044
  5.0 21.2 %copy-start.2 = (f32[32,8,128]{2,1,0:T(8,128)S(1)}, f32[32,8,128]{2,1,0:T(8,128)}, u32[]{:S(2)}) copy-start(f32[32,8,128]{2,1,0:T(8,128)} %param.13) | copy-start | bytes 393220
  16.2 10.0 %collective-permute-start.1 = (f32[1024,128]{1,0:T(8,128)S(1)}, f32[1024,128]{1,0:T(8,128)S(1)}, u32[]{:S(2)}, u32[]{:S(2)}) collective-permute-start(f32[1024,128]{1,0:T(8,128)S(1)} %bitcast.23), channel_id=1, source_target_pairs={{0,1},{1,0},{2,3},{3,2},{4,5},{5,4},{6,7},{7,6},{8,9},{9,8},{10,11... | collective-permute-start | bytes 1572872 | tf_op jit(solution)/shard_map/ppermute | solution.py:200
  51.2 1.9 %collective-permute-start.2 = (f32[512,128]{1,0:T(8,128)S(1)}, f32[512,128]{1,0:T(8,128)S(1)}, u32[]{:S(2)}, u32[]{:S(2)}) collective-permute-start(f32[512,128]{1,0:T(8,128)S(1)} %bitcast.25), channel_id=1, source_target_pairs={{0,1},{1,0},{2,3},{3,2},{4,5},{5,4},{6,7},{7,6},{8,9},{9,8},{10,11... | collective-permute-start | bytes 786440 | tf_op jit(solution)/shard_map/ppermute | solution.py:200
  53.8 18.0 %copy-start.3 = (f32[128,128]{1,0:T(8,128)S(1)}, f32[128,128]{1,0:T(8,128)}, u32[]{:S(2)}) copy-start(f32[128,128]{1,0:T(8,128)} %weight_ref.3) | copy-start | bytes 196612

commit v4 on v3

--- a/solution.py
+++ b/solution.py
@@ -24,6 +24,14 @@
     dot = functools.partial(
         lax.dot_general, dimension_numbers=dims, preferred_element_type=jnp.float32
     )
+    if left[0].shape[1] == LANES:
+        return dot(
+            jnp.concatenate([left[0], left[1], left[0]], axis=1),
+            jnp.concatenate([right[0], right[0], right[1]], axis=1 if transposed else 0),
+        )
+    if right[0].shape[1] == LANES and not transposed:
+        both = dot(left[0], jnp.concatenate([right[0], right[1]], axis=1))
+        return both[:, :LANES] + (both[:, LANES:] + dot(left[1], right[0]))
     return dot(left[0], right[0]) + (dot(left[0], right[1]) + dot(left[1], right[0]))
 
 
@@ -44,16 +52,15 @@
     return a, b, c, d
 
 
-def pack_kernel(core_ref, kept_ref, got_ref, vectors_ref, out_ref, vectors_out_ref):
-    vectors_out_ref[...] = vectors_ref[...]
+def pack_kernel(core_ref, kept_ref, left_ref, right_ref, out_ref):
     first_core = core_ref[0] == 0
 
-    def ordered(ref):
-        left = [ref[pl.ds(p, 32, stride=2), :] for p in range(2)]
-        right = [ref[pl.ds(q, 16, stride=4), :] for q in range(4)]
+    def ordered(left_ref, right_ref):
+        left = [left_ref[pl.ds(p, 32, stride=2), :] for p in range(2)]
+        right = [right_ref[pl.ds(q, 16, stride=4), :] for q in range(4)]
         return jnp.where(first_core, jnp.concatenate(left, axis=0), jnp.concatenate(right, axis=0))
 
-    kept, got = ordered(kept_ref), ordered(got_ref)
+    kept, got = ordered(kept_ref, kept_ref), ordered(left_ref, right_ref)
     lower, upper = jnp.where(first_core, kept, got), jnp.where(first_core, got, kept)
     block = jnp.concatenate([lower, upper], axis=1)
     for n in range(16):
@@ -88,12 +95,12 @@
         jnp.concatenate([right_scratch[pl.ds(j, 32, stride=8), :] for j in range(8)], axis=0)
     )
     left = jnp.where(first_core, own_ref[...], other_ref[...])
-    outer = product(split(left), right, True)
-    for wide in range(2):
-        for group in range(8):
+    outer = [product(split(left[n * 512 : (n + 1) * 512]), right, True) for n in range(2)]
+    for group in range(8):
+        for wide in range(2):
             blocks = [
-                outer[
-                    (group * 4 + p) * 32 : (group * 4 + p + 1) * 32,
+                outer[group // 4][
+                    (group % 4 * 4 + p) * 32 : (group % 4 * 4 + p + 1) * 32,
                     wide * LANES : (wide + 1) * LANES,
                 ]
                 for p in range(4)
@@ -249,7 +256,6 @@
     left = alignment_left.transpose(1, 2, 0).reshape(64, 64)
     right = alignment_right.transpose(1, 2, 0).reshape(64, 64)
     kept = jnp.where(core == 0, left, right)
-    got = exchange(jnp.where(core == 0, right, left), "seq", 1)
     vectors = [
         outer_mean_bias,
         input_norm_gain,
@@ -260,14 +266,14 @@
         input_bias_vector,
     ]
     vectors = jnp.concatenate([vector.reshape(-1, LANES) for vector in vectors], axis=0)
-    blocks, vectors = call(
+    (blocks,) = call(
         pack_kernel,
-        [(1024, LANES), vectors.shape],
+        [(1024, LANES)],
         [],
         [core_array],
         kept,
-        got,
-        vectors,
+        exchange(left, "seq", 1),
+        exchange(right, "seq", 1),
     )
     own = spread(blocks, gather_groups(rows, columns))
     send, updated, gate = call(

time: 73.1 us -> 71.6 us (0.979)
  Pallas kernels: 5.14 us -> 4.07 us
    pallas_call x4, Pallas kernels: 5.14 us -> 4.07 us  [call(): pl.pallas_call(kernel, out_shape=[jax.ShapeDtypeStruct(shape, jnp.float32...]
    ppermute x3 -> x4, waiting for transfers between devices: 2.63 us -> 2.41 us  [exchange(): return lax.ppermute(value, axis, [(n, n ^ distance) for n in range(count)])]
    ppermute x3 -> x4, starting transfers between devices: 12.5 us -> 12.3 us  [exchange(): return lax.ppermute(value, axis, [(n, n ^ distance) for n in range(count)])]
  transfers between devices with their start and end apart: 3 -> 4, of which waited for: 2 -> 4; matrix products, arithmetic and copies ran while one was open for 0% -> 1% of each run, Pallas kernels for 0% -> 0%
where the time goes in v4:
time: 71.6 us; the launch traced here: 71.3 us
  blocking collectives  50.7 us (71%)
  starting transfers between devices  12.3 us (17%)
  Pallas kernels  4.07 us (6%)
  waiting for transfers between devices  2.41 us (3%)
  local copies, waits for them, and re-layouts  0.85 us (1%)
  other arithmetic  0.84 us (1%)
    all_to_all x3, blocking collectives, spread(): lax.all_to_all(value, ('row', 'col', 'seq'), 0, 0, tiled=True, axis_index...  50.7 us
    ppermute x4, starting transfers between devices, exchange(): return lax.ppermute(value, axis, [(n, n ^ distance) for n in range(count)])  12.3 us
    pallas_call x4, Pallas kernels, call(): pl.pallas_call(kernel, out_shape=[jax.ShapeDtypeStruct(shape, jnp.float32...  4.07 us
    ppermute x4, waiting for transfers between devices, exchange(): return lax.ppermute(value, axis, [(n, n ^ distance) for n in range(count)])  2.41 us
  transfers between devices with their start and end apart: 4, of which 4 were waited for; matrix products, arithmetic and copies ran while one was open for 1% of the time, Pallas kernels for 0%

profile of v4, /device:TPU:1, one launch (start us, length us, event | category | flops | bytes accessed | tf_op | source)
XLA Modules:
  0.0 71.3 jit_solution(14418296464612571779)
XLA Ops:
  0.0 3.2 %collective-permute-start = (f32[64,64]{1,0:T(8,128)}, f32[64,64]{1,0:T(8,128)S(1)}, u32[]{:S(2)}, u32[]{:S(2)}) collective-permute-start(f32[64,64]{1,0:T(8,128)} %bitcast.32), channel_id=1, source_target_pairs={{0,1},{1,0},{2,3},{3,2},{4,5},{5,4},{6,7},{7,6},{8,9},{9,8},{10,11... | collective-permute-start | bytes 49160 | tf_op jit(solution)/shard_map/ppermute | solution.py:207
  3.2 0.8 %broadcast_select_fusion.kept_ref = f32[64,64]{1,0:T(8,128)S(1)} fusion(f32[64,64]{1,0:T(8,128)} %bitcast.33, f32[64,64]{1,0:T(8,128)} %bitcast.35, pred[]{:T(512)S(6)} %eq.5), kind=kLoop, calls=%fused_computation | loop fusion | flops 4096 | bytes 49153 | tf_op jit(solution)/shard_map/jit(_where)/select_n | solution.py:258
  4.0 0.3 collective-permute-done.left_ref
  4.3 0.3 collective-permute-done.1.right_ref
  4.7 0.1 shard_map.127
  4.8 0.0 copy-start
  4.8 0.0 copy-start.2
  4.8 11.2 %all_to_all.33 = f32[16,64,128]{2,1,0:T(8,128)S(1)} all-to-all(f32[16,64,128]{2,1,0:T(8,128)S(1)} %bitcast.25), channel_id=1, replica_groups={{20,22,16,18,28,30,24,26,4,6,0,2,12,14,8,10},{52,54,48,50,60,62,56,58,3..., dimensions={0} | all-to-all | bytes 1048576 | tf_op jit(solution)/shard_map/all_to_all | solution.py:249
  16.0 8.3 %collective-permute-start.2 = (f32[1024,128]{1,0:T(8,128)S(1)}, f32[1024,128]{1,0:T(8,128)S(1)}, u32[]{:S(2)}, u32[]{:S(2)}) collective-permute-start(f32[1024,128]{1,0:T(8,128)S(1)} %bitcast.23), channel_id=1, source_target_pairs={{0,1},{1,0},{2,3},{3,2},{4,5},{5,4},{6,7},{7,6},{8,9},{9,8},{10,11... | collective-permute-start | bytes 1572872 | tf_op jit(solution)/shard_map/ppermute | solution.py:207
  24.3 0.6 copy-done.8
  24.9 0.0 copy-done.9
  25.0 0.0 copy-done.10
  25.0 0.0 copy-done.4
  25.0 0.0 copy-done.7
  25.0 0.1 concatenate.3.vectors_ref
  25.2 0.1 pad_add_fusion.place_ref
  25.2 0.6 collective-permute-done.2.other_ref
  25.8 2.3 %shard_map.128 = (f32[512,128]{1,0:T(8,128)S(1)}, f32[256,128]{1,0:T(8,128)S(1)}, f32[256,128]{1,0:T(8,128)S(1)}) custom-call(s32[2]{0:T(128)S(1)} %pad_add_fusion.place_ref, f32[1024,128]{1,0:T(8,128)S(1)} %bitcast.24, f32[1024,128]{1,0:T(8,128)S(1)} %collective-permute-done.2.other_ref, f32[256,128]{1,0:T(8,128)S(1)} %bitcast.31, f32[1024,128]{1,0:T(8,128)S(1)} %copy-done, ...), custom_call_target="tpu_custom_call" | custom-call | tf_op jit(solution)/shard_map/pallas_call | solution.py:195
  28.1 21.6 %all_to_all.34 = f32[128,4,128]{2,1,0:T(4,128)S(1)} all-to-all(f32[128,4,128]{2,1,0:T(4,128)S(1)} %bitcast.30), channel_id=1, replica_groups={{148,150,144,146,156,158,152,154,132,134,128,130,140,142,136,138,180,18..., dimensions={0} | all-to-all | bytes 524288 | tf_op jit(solution)/shard_map/all_to_all | solution.py:249
  49.7 0.7 %collective-permute-start.3 = (f32[512,128]{1,0:T(8,128)S(1)}, f32[512,128]{1,0:T(8,128)S(1)}, u32[]{:S(2)}, u32[]{:S(2)}) collective-permute-start(f32[512,128]{1,0:T(8,128)S(1)} %bitcast.26), channel_id=1, source_target_pairs={{0,1},{1,0},{2,3},{3,2},{4,5},{5,4},{6,7},{7,6},{8,9},{9,8},{10,11... | collective-permute-start | bytes 786440 | tf_op jit(solution)/shard_map/ppermute | solution.py:207
  50.4 1.2 %collective-permute-done.3.other_ref = f32[512,128]{1,0:T(8,128)S(1)} collective-permute-done((f32[512,128]{1,0:T(8,128)S(1)}, f32[512,128]{1,0:T(8,128)S(1)}, u32[]{:S(2)}, u32[]{:S(2)}) %collective-permute-start.3) | collective-permute-done | bytes 262176 | tf_op jit(solution)/shard_map/ppermute | solution.py:207
  51.5 0.7 shard_map.129
  52.3 18.0 %all_to_all.35 = f32[128,2,128]{2,1,0:T(2,128)S(1)} all-to-all(f32[128,2,128]{2,1,0:T(2,128)S(1)} %bitcast.29), channel_id=1, replica_groups={{148,150,144,146,156,158,152,154,132,134,128,130,140,142,136,138,180,18..., dimensions={0} | all-to-all | bytes 262144 | tf_op jit(solution)/shard_map/all_to_all | solution.py:249
  70.3 1.0 %shard_map.130 = f32[256,128]{1,0:T(8,128)} custom-call(f32[256,128]{1,0:T(8,128)S(1)} %bitcast.28, f32[256,128]{1,0:T(8,128)S(1)} %get-tuple-element.9.updated_ref, f32[256,128]{1,0:T(8,128)S(1)} %get-tuple-element.10.gate_ref, f32[128,128]{1,0:T(8,128)S(1)} %copy-done.3, f32[11,128]{1,0:T(8,128)S(1)} %concatenate.3.vectors_ref), custom_call_target="tpu_custom_call" | custom-call | tf_op jit(solution)/shard_map/pallas_call | solution.py:195
  (16 shorter events, 0.0 us)
Async XLA Ops:
  0.0 4.3 %collective-permute-start = (f32[64,64]{1,0:T(8,128)}, f32[64,64]{1,0:T(8,128)S(1)}, u32[]{:S(2)}, u32[]{:S(2)}) collective-permute-start(f32[64,64]{1,0:T(8,128)} %bitcast.32), channel_id=1, source_target_pairs={{0,1},{1,0},{2,3},{3,2},{4,5},{5,4},{6,7},{7,6},{8,9},{9,8},{10,11... | collective-permute-start | bytes 49160 | tf_op jit(solution)/shard_map/ppermute | solution.py:207
  3.2 1.4 %collective-permute-start.1 = (f32[64,64]{1,0:T(8,128)}, f32[64,64]{1,0:T(8,128)S(1)}, u32[]{:S(2)}, u32[]{:S(2)}) collective-permute-start(f32[64,64]{1,0:T(8,128)} %bitcast.34), channel_id=1, source_target_pairs={{0,1},{1,0},{2,3},{3,2},{4,5},{5,4},{6,7},{7,6},{8,9},{9,8},{10,11... | collective-permute-start | bytes 49160 | tf_op jit(solution)/shard_map/ppermute | solution.py:207
  4.8 21.0 %copy-start = (f32[1024,128]{1,0:T(8,128)S(1)}, f32[1024,128]{1,0:T(8,128)}, u32[]{:S(2)}) copy-start(f32[1024,128]{1,0:T(8,128)} %mean_weight_ref.1) | copy-start | bytes 1572868
  4.8 21.0 %copy-start.1 = (f32[128,640]{1,0:T(8,128)S(1)}, f32[128,640]{1,0:T(8,128)}, u32[]{:S(2)}) copy-start(f32[128,640]{1,0:T(8,128)} %weight_ref.2) | copy-start | bytes 983044
  4.8 21.0 %copy-start.2 = (f32[32,8,128]{2,1,0:T(8,128)S(1)}, f32[32,8,128]{2,1,0:T(8,128)}, u32[]{:S(2)}) copy-start(f32[32,8,128]{2,1,0:T(8,128)} %param.13) | copy-start | bytes 393220
  16.0 9.8 %collective-permute-start.2 = (f32[1024,128]{1,0:T(8,128)S(1)}, f32[1024,128]{1,0:T(8,128)S(1)}, u32[]{:S(2)}, u32[]{:S(2)}) collective-permute-start(f32[1024,128]{1,0:T(8,128)S(1)} %bitcast.23), channel_id=1, source_target_pairs={{0,1},{1,0},{2,3},{3,2},{4,5},{5,4},{6,7},{7,6},{8,9},{9,8},{10,11... | collective-permute-start | bytes 1572872 | tf_op jit(solution)/shard_map/ppermute | solution.py:207
  24.3 0.7 copy-start.8
  24.3 0.7 copy-start.9
  24.3 0.7 copy-start.10
  24.3 0.7 %copy-start.4 = (f32[640]{0:T(1024)S(1)}, f32[640]{0:T(1024)}, u32[]{:S(2)}) copy-start(f32[640]{0:T(1024)} %param.21) | copy-start | bytes 7684
  24.3 0.7 %copy-start.5 = (f32[128]{0:T(128)S(1)}, f32[128]{0:T(128)}, u32[]{:S(2)}) copy-start(f32[128]{0:T(128)} %param.17) | copy-start | bytes 1540
  24.3 0.7 %copy-start.6 = (f32[128]{0:T(128)S(1)}, f32[128]{0:T(128)}, u32[]{:S(2)}) copy-start(f32[128]{0:T(128)} %param.18) | copy-start | bytes 1540
  24.3 0.7 %copy-start.7 = (f32[128]{0:T(128)S(1)}, f32[128]{0:T(128)}, u32[]{:S(2)}) copy-start(f32[128]{0:T(128)} %param.19) | copy-start | bytes 1540
  49.7 1.9 %collective-permute-start.3 = (f32[512,128]{1,0:T(8,128)S(1)}, f32[512,128]{1,0:T(8,128)S(1)}, u32[]{:S(2)}, u32[]{:S(2)}) collective-permute-start(f32[512,128]{1,0:T(8,128)S(1)} %bitcast.26), channel_id=1, source_target_pairs={{0,1},{1,0},{2,3},{3,2},{4,5},{5,4},{6,7},{7,6},{8,9},{9,8},{10,11... | collective-permute-start | bytes 786440 | tf_op jit(solution)/shard_map/ppermute | solution.py:207
  52.3 18.0 %copy-start.3 = (f32[128,128]{1,0:T(8,128)S(1)}, f32[128,128]{1,0:T(8,128)}, u32[]{:S(2)}) copy-start(f32[128,128]{1,0:T(8,128)} %weight_ref.3) | copy-start | bytes 196612

commit v5 on v4

--- a/solution.py
+++ b/solution.py
@@ -58,7 +58,7 @@
     def ordered(left_ref, right_ref):
         left = [left_ref[pl.ds(p, 32, stride=2), :] for p in range(2)]
         right = [right_ref[pl.ds(q, 16, stride=4), :] for q in range(4)]
-        return jnp.where(first_core, jnp.concatenate(left, axis=0), jnp.concatenate(right, axis=0))
+        return jnp.where(first_core, jnp.concatenate(right, axis=0), jnp.concatenate(left, axis=0))
 
     kept, got = ordered(kept_ref, kept_ref), ordered(left_ref, right_ref)
     lower, upper = jnp.where(first_core, kept, got), jnp.where(first_core, got, kept)
@@ -89,12 +89,12 @@
             start = odd * 512 + row * 64 + q * 16 + core * 8
             rows = pl.ds(pl.multiple_of(start, 8), 8)
             right_scratch[pl.ds((row ^ FAR_ROW) * 32 + q * 8, 8), :] = jnp.where(
-                first_core, other_ref[rows, :], own_ref[rows, :]
+                first_core, own_ref[rows, :], other_ref[rows, :]
             )
     right = split(
         jnp.concatenate([right_scratch[pl.ds(j, 32, stride=8), :] for j in range(8)], axis=0)
     )
-    left = jnp.where(first_core, own_ref[...], other_ref[...])
+    left = jnp.where(first_core, other_ref[...], own_ref[...])
     outer = [product(split(left[n * 512 : (n + 1) * 512]), right, True) for n in range(2)]
     for group in range(8):
         for wide in range(2):
@@ -219,10 +219,10 @@
 def gather_groups(rows, columns):
     place = lambda row, column, core: (row * columns + column) * 2 + core
     first = [
-        [place(row, column ^ FAR_COLUMN, 0) for column in range(columns)] for row in range(rows)
+        [place(row, column ^ FAR_COLUMN, 1) for column in range(columns)] for row in range(rows)
     ]
     second = [
-        [place(row ^ FAR_ROW, column + n, 1) for n in range(2) for row in range(rows)]
+        [place(row ^ FAR_ROW, column + n, 0) for n in range(2) for row in range(rows)]
         for column in range(0, columns, 2)
     ]
     return first + second
@@ -255,7 +255,7 @@
     core_array = core.reshape(1)
     left = alignment_left.transpose(1, 2, 0).reshape(64, 64)
     right = alignment_right.transpose(1, 2, 0).reshape(64, 64)
-    kept = jnp.where(core == 0, left, right)
+    kept = jnp.where(core == 0, right, left)
     vectors = [
         outer_mean_bias,
         input_norm_gain,

time: 71.6 us -> 71.1 us (level)
  starting transfers between devices: 12.3 us -> 3.95 us
  blocking collectives: 50.7 us -> 58.2 us
    ppermute x4, starting transfers between devices: 12.3 us -> 3.95 us  [exchange(): return lax.ppermute(value, axis, [(n, n ^ distance) for n in range(count)])]
    all_to_all x3, blocking collectives: 50.7 us -> 58.2 us  [spread(): lax.all_to_all(value, ('row', 'col', 'seq'), 0, 0, tiled=True, axis_index...]
where the time goes in v5:
time: 71.1 us; the launch traced here: 70.8 us
  blocking collectives  58.2 us (82%)
  Pallas kernels  4.07 us (6%)
  starting transfers between devices  3.95 us (6%)
  waiting for transfers between devices  2.77 us (4%)
  other arithmetic  0.84 us (1%)
  local copies, waits for them, and re-layouts  0.83 us (1%)
    all_to_all x3, blocking collectives, spread(): lax.all_to_all(value, ('row', 'col', 'seq'), 0, 0, tiled=True, axis_index...  58.2 us
    pallas_call x4, Pallas kernels, call(): pl.pallas_call(kernel, out_shape=[jax.ShapeDtypeStruct(shape, jnp.float32...  4.07 us
    ppermute x4, starting transfers between devices, exchange(): return lax.ppermute(value, axis, [(n, n ^ distance) for n in range(count)])  3.95 us
    ppermute x4, waiting for transfers between devices, exchange(): return lax.ppermute(value, axis, [(n, n ^ distance) for n in range(count)])  2.77 us
  transfers between devices with their start and end apart: 4, of which 4 were waited for; matrix products, arithmetic and copies ran while one was open for 1% of the time, Pallas kernels for 0%

profile of v5, /device:TPU:1, one launch (start us, length us, event | category | flops | bytes accessed | tf_op | source)
XLA Modules:
  0.0 70.8 jit_solution(6747706413380733546)
XLA Ops:
  0.0 3.2 %collective-permute-start = (f32[64,64]{1,0:T(8,128)}, f32[64,64]{1,0:T(8,128)S(1)}, u32[]{:S(2)}, u32[]{:S(2)}) collective-permute-start(f32[64,64]{1,0:T(8,128)} %bitcast.32), channel_id=1, source_target_pairs={{0,1},{1,0},{2,3},{3,2},{4,5},{5,4},{6,7},{7,6},{8,9},{9,8},{10,11... | collective-permute-start | bytes 49160 | tf_op jit(solution)/shard_map/ppermute | solution.py:207
  3.2 0.8 %broadcast_select_fusion.kept_ref = f32[64,64]{1,0:T(8,128)S(1)} fusion(f32[64,64]{1,0:T(8,128)} %bitcast.35, f32[64,64]{1,0:T(8,128)} %bitcast.33, pred[]{:T(512)S(6)} %eq.5), kind=kLoop, calls=%fused_computation | loop fusion | flops 4096 | bytes 49153 | tf_op jit(solution)/shard_map/jit(_where)/select_n | solution.py:258
  4.0 0.3 collective-permute-done.left_ref
  4.3 0.3 collective-permute-done.1.right_ref
  4.7 0.1 shard_map.127
  4.8 0.0 copy-start
  4.8 0.0 copy-start.1
  4.8 17.1 %all_to_all.33 = f32[16,64,128]{2,1,0:T(8,128)S(1)} all-to-all(f32[16,64,128]{2,1,0:T(8,128)S(1)} %bitcast.25), channel_id=1, replica_groups={{21,23,17,19,29,31,25,27,5,7,1,3,13,15,9,11},{53,55,49,51,61,63,57,59,3..., dimensions={0} | all-to-all | bytes 1048576 | tf_op jit(solution)/shard_map/all_to_all | solution.py:249
  22.0 0.0 copy-start.4
  22.0 0.6 copy-done.8
  22.6 0.0 copy-done.9
  22.6 0.0 copy-done.10
  22.6 0.0 copy-done.4
  22.7 0.0 copy-done.7
  22.7 0.1 concatenate.3.vectors_ref
  22.8 0.1 pad_add_fusion.place_ref
  22.9 1.0 %collective-permute-done.2.other_ref = f32[1024,128]{1,0:T(8,128)S(1)} collective-permute-done((f32[1024,128]{1,0:T(8,128)S(1)}, f32[1024,128]{1,0:T(8,128)S(1)}, u32[]{:S(2)}, u32[]{:S(2)}) %collective-permute-start.2) | collective-permute-done | bytes 524320 | tf_op jit(solution)/shard_map/ppermute | solution.py:207
  23.9 2.3 %shard_map.128 = (f32[512,128]{1,0:T(8,128)S(1)}, f32[256,128]{1,0:T(8,128)S(1)}, f32[256,128]{1,0:T(8,128)S(1)}) custom-call(s32[2]{0:T(128)S(1)} %pad_add_fusion.place_ref, f32[1024,128]{1,0:T(8,128)S(1)} %bitcast.24, f32[1024,128]{1,0:T(8,128)S(1)} %collective-permute-done.2.other_ref, f32[256,128]{1,0:T(8,128)S(1)} %bitcast.31, f32[1024,128]{1,0:T(8,128)S(1)} %copy-done, ...), custom_call_target="tpu_custom_call" | custom-call | tf_op jit(solution)/shard_map/pallas_call | solution.py:195
  26.1 23.1 %all_to_all.34 = f32[128,4,128]{2,1,0:T(4,128)S(1)} all-to-all(f32[128,4,128]{2,1,0:T(4,128)S(1)} %bitcast.30), channel_id=1, replica_groups={{148,150,144,146,156,158,152,154,132,134,128,130,140,142,136,138,180,18..., dimensions={0} | all-to-all | bytes 524288 | tf_op jit(solution)/shard_map/all_to_all | solution.py:249
  49.2 0.7 collective-permute-start.3
  49.9 1.2 %collective-permute-done.3.other_ref = f32[512,128]{1,0:T(8,128)S(1)} collective-permute-done((f32[512,128]{1,0:T(8,128)S(1)}, f32[512,128]{1,0:T(8,128)S(1)}, u32[]{:S(2)}, u32[]{:S(2)}) %collective-permute-start.3) | collective-permute-done | bytes 262176 | tf_op jit(solution)/shard_map/ppermute | solution.py:207
  51.0 0.7 %shard_map.129 = f32[256,128]{1,0:T(8,128)S(1)} custom-call(s32[1]{0:T(128)} %bitcast.core_ref, f32[512,128]{1,0:T(8,128)S(1)} %bitcast.27, f32[512,128]{1,0:T(8,128)S(1)} %collective-permute-done.3.other_ref), custom_call_target="tpu_custom_call" | custom-call | tf_op jit(solution)/shard_map/pallas_call | solution.py:195
  51.8 18.0 %all_to_all.35 = f32[128,2,128]{2,1,0:T(2,128)S(1)} all-to-all(f32[128,2,128]{2,1,0:T(2,128)S(1)} %bitcast.29), channel_id=1, replica_groups={{148,150,144,146,156,158,152,154,132,134,128,130,140,142,136,138,180,18..., dimensions={0} | all-to-all | bytes 262144 | tf_op jit(solution)/shard_map/all_to_all | solution.py:249
  69.8 1.0 %shard_map.130 = f32[256,128]{1,0:T(8,128)} custom-call(f32[256,128]{1,0:T(8,128)S(1)} %bitcast.28, f32[256,128]{1,0:T(8,128)S(1)} %get-tuple-element.9.updated_ref, f32[256,128]{1,0:T(8,128)S(1)} %get-tuple-element.10.gate_ref, f32[128,128]{1,0:T(8,128)S(1)} %copy-done.3, f32[11,128]{1,0:T(8,128)S(1)} %concatenate.3.vectors_ref), custom_call_target="tpu_custom_call" | custom-call | tf_op jit(solution)/shard_map/pallas_call | solution.py:195
  (16 shorter events, 0.0 us)
Async XLA Ops:
  0.0 4.3 %collective-permute-start = (f32[64,64]{1,0:T(8,128)}, f32[64,64]{1,0:T(8,128)S(1)}, u32[]{:S(2)}, u32[]{:S(2)}) collective-permute-start(f32[64,64]{1,0:T(8,128)} %bitcast.32), channel_id=1, source_target_pairs={{0,1},{1,0},{2,3},{3,2},{4,5},{5,4},{6,7},{7,6},{8,9},{9,8},{10,11... | collective-permute-start | bytes 49160 | tf_op jit(solution)/shard_map/ppermute | solution.py:207
  3.2 1.4 %collective-permute-start.1 = (f32[64,64]{1,0:T(8,128)}, f32[64,64]{1,0:T(8,128)S(1)}, u32[]{:S(2)}, u32[]{:S(2)}) collective-permute-start(f32[64,64]{1,0:T(8,128)} %bitcast.34), channel_id=1, source_target_pairs={{0,1},{1,0},{2,3},{3,2},{4,5},{5,4},{6,7},{7,6},{8,9},{9,8},{10,11... | collective-permute-start | bytes 49160 | tf_op jit(solution)/shard_map/ppermute | solution.py:207
  4.8 19.1 %copy-start = (f32[1024,128]{1,0:T(8,128)S(1)}, f32[1024,128]{1,0:T(8,128)}, u32[]{:S(2)}) copy-start(f32[1024,128]{1,0:T(8,128)} %mean_weight_ref.1) | copy-start | bytes 1572868
  4.8 19.1 %copy-start.1 = (f32[128,640]{1,0:T(8,128)S(1)}, f32[128,640]{1,0:T(8,128)}, u32[]{:S(2)}) copy-start(f32[128,640]{1,0:T(8,128)} %weight_ref.2) | copy-start | bytes 983044
  4.8 19.0 %copy-start.2 = (f32[32,8,128]{2,1,0:T(8,128)S(1)}, f32[32,8,128]{2,1,0:T(8,128)}, u32[]{:S(2)}) copy-start(f32[32,8,128]{2,1,0:T(8,128)} %param.13) | copy-start | bytes 393220
  21.9 1.9 %collective-permute-start.2 = (f32[1024,128]{1,0:T(8,128)S(1)}, f32[1024,128]{1,0:T(8,128)S(1)}, u32[]{:S(2)}, u32[]{:S(2)}) collective-permute-start(f32[1024,128]{1,0:T(8,128)S(1)} %bitcast.23), channel_id=1, source_target_pairs={{0,1},{1,0},{2,3},{3,2},{4,5},{5,4},{6,7},{7,6},{8,9},{9,8},{10,11... | collective-permute-start | bytes 1572872 | tf_op jit(solution)/shard_map/ppermute | solution.py:207
  21.9 0.7 copy-start.8
  21.9 0.7 copy-start.9
  21.9 0.7 copy-start.10
  22.0 0.7 %copy-start.4 = (f32[640]{0:T(1024)S(1)}, f32[640]{0:T(1024)}, u32[]{:S(2)}) copy-start(f32[640]{0:T(1024)} %param.21) | copy-start | bytes 7684
  22.0 0.7 %copy-start.5 = (f32[128]{0:T(128)S(1)}, f32[128]{0:T(128)}, u32[]{:S(2)}) copy-start(f32[128]{0:T(128)} %param.17) | copy-start | bytes 1540
  22.0 0.7 copy-start.6
  22.0 0.7 copy-start.7
  49.2 1.9 %collective-permute-start.3 = (f32[512,128]{1,0:T(8,128)S(1)}, f32[512,128]{1,0:T(8,128)S(1)}, u32[]{:S(2)}, u32[]{:S(2)}) collective-permute-start(f32[512,128]{1,0:T(8,128)S(1)} %bitcast.26), channel_id=1, source_target_pairs={{0,1},{1,0},{2,3},{3,2},{4,5},{5,4},{6,7},{7,6},{8,9},{9,8},{10,11... | collective-permute-start | bytes 786440 | tf_op jit(solution)/shard_map/ppermute | solution.py:207
  51.8 18.0 %copy-start.3 = (f32[128,128]{1,0:T(8,128)S(1)}, f32[128,128]{1,0:T(8,128)}, u32[]{:S(2)}) copy-start(f32[128,128]{1,0:T(8,128)} %weight_ref.3) | copy-start | bytes 196612

commit v6 on v5

--- a/solution.py
+++ b/solution.py
@@ -11,7 +11,7 @@
 EPSILON = 1e-05
 LANES = 128
 VMEM_LIMIT = 32 * 1024 * 1024
-FAR_ROW, FAR_COLUMN = 4, 10
+GATHER_ROW, OUT_ROW, BACK_ROW, FAR_COLUMN = 5, 7, 6, 10
 
 
 def split(value):
@@ -88,7 +88,7 @@
         for q in range(4):
             start = odd * 512 + row * 64 + q * 16 + core * 8
             rows = pl.ds(pl.multiple_of(start, 8), 8)
-            right_scratch[pl.ds((row ^ FAR_ROW) * 32 + q * 8, 8), :] = jnp.where(
+            right_scratch[pl.ds((row ^ GATHER_ROW) * 32 + q * 8, 8), :] = jnp.where(
                 first_core, own_ref[rows, :], other_ref[rows, :]
             )
     right = split(
@@ -126,10 +126,13 @@
     ]
     left_act = jnp.transpose(jax.nn.sigmoid(blocks[1]) * blocks[0])
     right_act = jnp.transpose(jax.nn.sigmoid(blocks[3]) * blocks[2])
-    send_ref[pl.ds(0, 128, stride=4), :] = left_act[:, :LANES]
-    send_ref[pl.ds(1, 128, stride=4), :] = left_act[:, LANES:]
-    send_ref[pl.ds(2, 128, stride=4), :] = right_act[:, :LANES]
-    send_ref[pl.ds(3, 128, stride=4), :] = right_act[:, LANES:]
+    for n in range(8):
+        channels = slice(n * 16, (n + 1) * 16)
+        begin = (n ^ OUT_ROW ^ BACK_ROW) * 64
+        send_ref[pl.ds(begin, 16, stride=4), :] = left_act[channels, :LANES]
+        send_ref[pl.ds(begin + 1, 16, stride=4), :] = left_act[channels, LANES:]
+        send_ref[pl.ds(begin + 2, 16, stride=4), :] = right_act[channels, :LANES]
+        send_ref[pl.ds(begin + 3, 16, stride=4), :] = right_act[channels, LANES:]
     gate_ref[...] = jax.nn.sigmoid(blocks[4])
 
 
@@ -171,7 +174,7 @@
                 for g in range(4)
             ]
             for r, block in enumerate(swap_groups(blocks)):
-                place = (wide * 4 + r) ^ (FAR_COLUMN // 2) ^ FAR_ROW
+                place = (wide * 4 + r) ^ (FAR_COLUMN // 2) ^ BACK_ROW
                 send_ref[pl.ds(place * 32 + part, 16, stride=2), :] = block
 
 
@@ -207,13 +210,15 @@
     return lax.ppermute(value, axis, [(n, n ^ distance) for n in range(count)])
 
 
-def far_first(rows, columns):
-    return [(row ^ FAR_ROW, column ^ FAR_COLUMN) for row in range(rows) for column in range(columns)]
-
-
-def exchange_groups(rows, columns):
-    places = far_first(rows, columns)
-    return [[(row * columns + column) * 2 + core for row, column in places] for core in range(2)]
+def exchange_groups(rows, columns, mask):
+    return [
+        [
+            ((row ^ mask) * columns + (column ^ FAR_COLUMN)) * 2 + core
+            for row in range(rows)
+            for column in range(columns)
+        ]
+        for core in range(2)
+    ]
 
 
 def gather_groups(rows, columns):
@@ -222,7 +227,7 @@
         [place(row, column ^ FAR_COLUMN, 1) for column in range(columns)] for row in range(rows)
     ]
     second = [
-        [place(row ^ FAR_ROW, column + n, 0) for n in range(2) for row in range(rows)]
+        [place(row ^ GATHER_ROW, column + n, 0) for n in range(2) for row in range(rows)]
         for column in range(0, columns, 2)
     ]
     return first + second
@@ -292,7 +297,7 @@
         input_weight_matrix,
         vectors,
     )
-    own = spread(send, exchange_groups(rows, columns))
+    own = spread(send, exchange_groups(rows, columns, OUT_ROW))
     (back,) = call(
         triangle_kernel,
         [(256, LANES)],
@@ -304,7 +309,7 @@
         own,
         exchange(own, "seq", 1),
     )
-    mixed = spread(back, exchange_groups(rows, columns))
+    mixed = spread(back, exchange_groups(rows, columns, BACK_ROW))
     (out,) = call(
         output_kernel,
         [(256, LANES)],

time: 71.1 us -> 70.7 us (level)
  blocking collectives: 58.2 us -> 57 us
  starting transfers between devices: 3.95 us -> 4.69 us
    all_to_all x3, blocking collectives: 58.2 us -> 57 us  [spread(): lax.all_to_all(value, ('row', 'col', 'seq'), 0, 0, tiled=True, axis_index...]
    ppermute x4, starting transfers between devices: 3.95 us -> 4.69 us  [exchange(): return lax.ppermute(value, axis, [(n, n ^ distance) for n in range(count)])]
where the time goes in v6:
time: 70.7 us; the launch traced here: 70.4 us
  blocking collectives  57 us (81%)
  starting transfers between devices  4.69 us (7%)
  Pallas kernels  4.08 us (6%)
  waiting for transfers between devices  2.77 us (4%)
  other arithmetic  0.84 us (1%)
  local copies, waits for them, and re-layouts  0.83 us (1%)
    all_to_all x3, blocking collectives, spread(): lax.all_to_all(value, ('row', 'col', 'seq'), 0, 0, tiled=True, axis_index...  57 us
    ppermute x4, starting transfers between devices, exchange(): return lax.ppermute(value, axis, [(n, n ^ distance) for n in range(count)])  4.69 us
    pallas_call x4, Pallas kernels, call(): pl.pallas_call(kernel, out_shape=[jax.ShapeDtypeStruct(shape, jnp.float32...  4.08 us
    ppermute x4, waiting for transfers between devices, exchange(): return lax.ppermute(value, axis, [(n, n ^ distance) for n in range(count)])  2.77 us
  transfers between devices with their start and end apart: 4, of which 4 were waited for; matrix products, arithmetic and copies ran while one was open for 1% of the time, Pallas kernels for 0%

profile of v6, /device:TPU:1, one launch (start us, length us, event | category | flops | bytes accessed | tf_op | source)
XLA Modules:
  0.0 70.4 jit_solution(7961440410402479515)
XLA Ops:
  0.0 3.2 %collective-permute-start = (f32[64,64]{1,0:T(8,128)}, f32[64,64]{1,0:T(8,128)S(1)}, u32[]{:S(2)}, u32[]{:S(2)}) collective-permute-start(f32[64,64]{1,0:T(8,128)} %bitcast.32), channel_id=1, source_target_pairs={{0,1},{1,0},{2,3},{3,2},{4,5},{5,4},{6,7},{7,6},{8,9},{9,8},{10,11... | collective-permute-start | bytes 49160 | tf_op jit(solution)/shard_map/ppermute | solution.py:210
  3.2 0.8 %broadcast_select_fusion.kept_ref = f32[64,64]{1,0:T(8,128)S(1)} fusion(f32[64,64]{1,0:T(8,128)} %bitcast.35, f32[64,64]{1,0:T(8,128)} %bitcast.33, pred[]{:T(512)S(6)} %eq.5), kind=kLoop, calls=%fused_computation | loop fusion | flops 4096 | bytes 49153 | tf_op jit(solution)/shard_map/jit(_where)/select_n | solution.py:263
  4.0 0.3 collective-permute-done.left_ref
  4.3 0.3 collective-permute-done.1.right_ref
  4.7 0.1 shard_map.127
  4.8 0.0 copy-start.2
  4.8 17.1 %all_to_all.33 = f32[16,64,128]{2,1,0:T(8,128)S(1)} all-to-all(f32[16,64,128]{2,1,0:T(8,128)S(1)} %bitcast.25), channel_id=1, replica_groups={{21,23,17,19,29,31,25,27,5,7,1,3,13,15,9,11},{53,55,49,51,61,63,57,59,3..., dimensions={0} | all-to-all | bytes 1048576 | tf_op jit(solution)/shard_map/all_to_all | solution.py:254
  22.0 0.0 copy-start.4
  22.0 0.0 copy-start.5
  22.0 0.6 copy-done.8
  22.6 0.0 copy-done.9
  22.6 0.0 copy-done.10
  22.6 0.0 copy-done.4
  22.7 0.0 copy-done.7
  22.7 0.1 concatenate.3.vectors_ref
  22.8 0.1 pad_add_fusion.place_ref
  22.9 1.0 %collective-permute-done.2.other_ref = f32[1024,128]{1,0:T(8,128)S(1)} collective-permute-done((f32[1024,128]{1,0:T(8,128)S(1)}, f32[1024,128]{1,0:T(8,128)S(1)}, u32[]{:S(2)}, u32[]{:S(2)}) %collective-permute-start.2) | collective-permute-done | bytes 524320 | tf_op jit(solution)/shard_map/ppermute | solution.py:210
  23.9 2.3 %shard_map.128 = (f32[512,128]{1,0:T(8,128)S(1)}, f32[256,128]{1,0:T(8,128)S(1)}, f32[256,128]{1,0:T(8,128)S(1)}) custom-call(s32[2]{0:T(128)S(1)} %pad_add_fusion.place_ref, f32[1024,128]{1,0:T(8,128)S(1)} %bitcast.24, f32[1024,128]{1,0:T(8,128)S(1)} %collective-permute-done.2.other_ref, f32[256,128]{1,0:T(8,128)S(1)} %bitcast.31, f32[1024,128]{1,0:T(8,128)S(1)} %copy-done, ...), custom_call_target="tpu_custom_call" | custom-call | tf_op jit(solution)/shard_map/pallas_call | solution.py:198
  26.1 22.9 %all_to_all.34 = f32[128,4,128]{2,1,0:T(4,128)S(1)} all-to-all(f32[128,4,128]{2,1,0:T(4,128)S(1)} %bitcast.30), channel_id=1, replica_groups={{244,246,240,242,252,254,248,250,228,230,224,226,236,238,232,234,212,21..., dimensions={0} | all-to-all | bytes 524288 | tf_op jit(solution)/shard_map/all_to_all | solution.py:254
  49.0 1.4 %collective-permute-start.3 = (f32[512,128]{1,0:T(8,128)S(1)}, f32[512,128]{1,0:T(8,128)S(1)}, u32[]{:S(2)}, u32[]{:S(2)}) collective-permute-start(f32[512,128]{1,0:T(8,128)S(1)} %bitcast.26), channel_id=1, source_target_pairs={{0,1},{1,0},{2,3},{3,2},{4,5},{5,4},{6,7},{7,6},{8,9},{9,8},{10,11... | collective-permute-start | bytes 786440 | tf_op jit(solution)/shard_map/ppermute | solution.py:210
  50.4 1.2 %collective-permute-done.3.other_ref = f32[512,128]{1,0:T(8,128)S(1)} collective-permute-done((f32[512,128]{1,0:T(8,128)S(1)}, f32[512,128]{1,0:T(8,128)S(1)}, u32[]{:S(2)}, u32[]{:S(2)}) %collective-permute-start.3) | collective-permute-done | bytes 262176 | tf_op jit(solution)/shard_map/ppermute | solution.py:210
  51.6 0.7 %shard_map.129 = f32[256,128]{1,0:T(8,128)S(1)} custom-call(s32[1]{0:T(128)} %bitcast.core_ref, f32[512,128]{1,0:T(8,128)S(1)} %bitcast.27, f32[512,128]{1,0:T(8,128)S(1)} %collective-permute-done.3.other_ref), custom_call_target="tpu_custom_call" | custom-call | tf_op jit(solution)/shard_map/pallas_call | solution.py:198
  52.3 17.0 %all_to_all.35 = f32[128,2,128]{2,1,0:T(2,128)S(1)} all-to-all(f32[128,2,128]{2,1,0:T(2,128)S(1)} %bitcast.29), channel_id=1, replica_groups={{212,214,208,210,220,222,216,218,196,198,192,194,204,206,200,202,244,24..., dimensions={0} | all-to-all | bytes 262144 | tf_op jit(solution)/shard_map/all_to_all | solution.py:254
  69.4 1.0 %shard_map.130 = f32[256,128]{1,0:T(8,128)} custom-call(f32[256,128]{1,0:T(8,128)S(1)} %bitcast.28, f32[256,128]{1,0:T(8,128)S(1)} %get-tuple-element.9.updated_ref, f32[256,128]{1,0:T(8,128)S(1)} %get-tuple-element.10.gate_ref, f32[128,128]{1,0:T(8,128)S(1)} %copy-done.3, f32[11,128]{1,0:T(8,128)S(1)} %concatenate.3.vectors_ref), custom_call_target="tpu_custom_call" | custom-call | tf_op jit(solution)/shard_map/pallas_call | solution.py:198
  (16 shorter events, 0.0 us)
Async XLA Ops:
  0.0 4.3 %collective-permute-start = (f32[64,64]{1,0:T(8,128)}, f32[64,64]{1,0:T(8,128)S(1)}, u32[]{:S(2)}, u32[]{:S(2)}) collective-permute-start(f32[64,64]{1,0:T(8,128)} %bitcast.32), channel_id=1, source_target_pairs={{0,1},{1,0},{2,3},{3,2},{4,5},{5,4},{6,7},{7,6},{8,9},{9,8},{10,11... | collective-permute-start | bytes 49160 | tf_op jit(solution)/shard_map/ppermute | solution.py:210
  3.2 1.4 %collective-permute-start.1 = (f32[64,64]{1,0:T(8,128)}, f32[64,64]{1,0:T(8,128)S(1)}, u32[]{:S(2)}, u32[]{:S(2)}) collective-permute-start(f32[64,64]{1,0:T(8,128)} %bitcast.34), channel_id=1, source_target_pairs={{0,1},{1,0},{2,3},{3,2},{4,5},{5,4},{6,7},{7,6},{8,9},{9,8},{10,11... | collective-permute-start | bytes 49160 | tf_op jit(solution)/shard_map/ppermute | solution.py:210
  4.8 19.1 %copy-start = (f32[1024,128]{1,0:T(8,128)S(1)}, f32[1024,128]{1,0:T(8,128)}, u32[]{:S(2)}) copy-start(f32[1024,128]{1,0:T(8,128)} %mean_weight_ref.1) | copy-start | bytes 1572868
  4.8 19.1 %copy-start.1 = (f32[128,640]{1,0:T(8,128)S(1)}, f32[128,640]{1,0:T(8,128)}, u32[]{:S(2)}) copy-start(f32[128,640]{1,0:T(8,128)} %weight_ref.2) | copy-start | bytes 983044
  4.8 19.0 %copy-start.2 = (f32[32,8,128]{2,1,0:T(8,128)S(1)}, f32[32,8,128]{2,1,0:T(8,128)}, u32[]{:S(2)}) copy-start(f32[32,8,128]{2,1,0:T(8,128)} %param.13) | copy-start | bytes 393220
  21.9 1.9 %collective-permute-start.2 = (f32[1024,128]{1,0:T(8,128)S(1)}, f32[1024,128]{1,0:T(8,128)S(1)}, u32[]{:S(2)}, u32[]{:S(2)}) collective-permute-start(f32[1024,128]{1,0:T(8,128)S(1)} %bitcast.23), channel_id=1, source_target_pairs={{0,1},{1,0},{2,3},{3,2},{4,5},{5,4},{6,7},{7,6},{8,9},{9,8},{10,11... | collective-permute-start | bytes 1572872 | tf_op jit(solution)/shard_map/ppermute | solution.py:210
  21.9 0.7 copy-start.8
  21.9 0.7 copy-start.9
  21.9 0.7 copy-start.10
  22.0 0.7 %copy-start.4 = (f32[640]{0:T(1024)S(1)}, f32[640]{0:T(1024)}, u32[]{:S(2)}) copy-start(f32[640]{0:T(1024)} %param.21) | copy-start | bytes 7684
  22.0 0.7 %copy-start.5 = (f32[128]{0:T(128)S(1)}, f32[128]{0:T(128)}, u32[]{:S(2)}) copy-start(f32[128]{0:T(128)} %param.17) | copy-start | bytes 1540
  22.0 0.7 copy-start.6
  22.0 0.7 copy-start.7
  49.0 2.6 %collective-permute-start.3 = (f32[512,128]{1,0:T(8,128)S(1)}, f32[512,128]{1,0:T(8,128)S(1)}, u32[]{:S(2)}, u32[]{:S(2)}) collective-permute-start(f32[512,128]{1,0:T(8,128)S(1)} %bitcast.26), channel_id=1, source_target_pairs={{0,1},{1,0},{2,3},{3,2},{4,5},{5,4},{6,7},{7,6},{8,9},{9,8},{10,11... | collective-permute-start | bytes 786440 | tf_op jit(solution)/shard_map/ppermute | solution.py:210
  52.3 17.1 %copy-start.3 = (f32[128,128]{1,0:T(8,128)S(1)}, f32[128,128]{1,0:T(8,128)}, u32[]{:S(2)}) copy-start(f32[128,128]{1,0:T(8,128)} %weight_ref.3) | copy-start | bytes 196612

commit v7 on v6

--- a/solution.py
+++ b/solution.py
@@ -52,8 +52,8 @@
     return a, b, c, d
 
 
-def pack_kernel(core_ref, kept_ref, left_ref, right_ref, out_ref):
-    first_core = core_ref[0] == 0
+def pack_kernel(kept_ref, left_ref, right_ref, out_ref):
+    first_core = lax.axis_index("seq") == 0
 
     def ordered(left_ref, right_ref):
         left = [left_ref[pl.ds(p, 32, stride=2), :] for p in range(2)]
@@ -68,7 +68,6 @@
 
 
 def tile_kernel(
-    place_ref,
     own_ref,
     other_ref,
     pair_ref,
@@ -82,7 +81,7 @@
     high_scratch,
     low_scratch,
 ):
-    core, odd = place_ref[0], place_ref[1]
+    core, odd = lax.axis_index("seq"), lax.rem(lax.axis_index("col"), 2)
     first_core = core == 0
     for row in range(8):
         for q in range(4):
@@ -136,8 +135,8 @@
     gate_ref[...] = jax.nn.sigmoid(blocks[4])
 
 
-def triangle_kernel(core_ref, own_ref, other_ref, send_ref, left_scratch, right_scratch):
-    first_core = core_ref[0] == 0
+def triangle_kernel(own_ref, other_ref, send_ref, left_scratch, right_scratch):
+    first_core = lax.axis_index("seq") == 0
 
     def regroup(source, part, wide):
         return swap_groups([source(wide * 4 + r, part) for r in range(4)])
@@ -192,17 +191,15 @@
         out_ref[pl.ds(j, 32, stride=8), :] = out[j * 32 : (j + 1) * 32]
 
 
-def call(kernel, outputs, scratch, scalars, *blocks):
-    specs = [pl.BlockSpec(memory_space=pltpu.SMEM)] * len(scalars)
-    specs += [pl.BlockSpec(memory_space=pltpu.VMEM)] * len(blocks)
+def call(kernel, outputs, scratch, *blocks):
     return pl.pallas_call(
         kernel,
         out_shape=[jax.ShapeDtypeStruct(shape, jnp.float32) for shape in outputs],
-        in_specs=specs,
+        in_specs=[pl.BlockSpec(memory_space=pltpu.VMEM)] * len(blocks),
         out_specs=[pl.BlockSpec(memory_space=pltpu.VMEM)] * len(outputs),
         scratch_shapes=scratch,
         compiler_params=pltpu.CompilerParams(vmem_limit_bytes=VMEM_LIMIT),
-    )(*scalars, *blocks)
+    )(*blocks)
 
 
 def exchange(value, axis, distance):
@@ -256,8 +253,6 @@
         )
 
     core = lax.axis_index("seq")
-    place = jnp.stack([core, lax.axis_index("col") % 2])
-    core_array = core.reshape(1)
     left = alignment_left.transpose(1, 2, 0).reshape(64, 64)
     right = alignment_right.transpose(1, 2, 0).reshape(64, 64)
     kept = jnp.where(core == 0, right, left)
@@ -275,7 +270,6 @@
         pack_kernel,
         [(1024, LANES)],
         [],
-        [core_array],
         kept,
         exchange(left, "seq", 1),
         exchange(right, "seq", 1),
@@ -289,7 +283,6 @@
             pltpu.VMEM((256, 1024), jnp.bfloat16),
             pltpu.VMEM((256, 1024), jnp.bfloat16),
         ],
-        [place],
         own,
         exchange(own, "seq", 1),
         pair.reshape(256, LANES),
@@ -305,7 +298,6 @@
             pltpu.VMEM((2, 256, LANES), jnp.float32),
             pltpu.VMEM((2, 128, LANES), jnp.float32),
         ],
-        [core_array],
         own,
         exchange(own, "seq", 1),
     )
@@ -313,7 +305,6 @@
     (out,) = call(
         output_kernel,
         [(256, LANES)],
-        [],
         [],
         mixed,
         updated,

time: 70.7 us -> 70.2 us (level)
  no operation moved by 1% of the time
where the time goes in v7:
time: 70.2 us; the launch traced here: 69.9 us
  blocking collectives  57 us (81%)
  starting transfers between devices  4.69 us (7%)
  Pallas kernels  3.56 us (5%)
  waiting for transfers between devices  2.9 us (4%)
  local copies, waits for them, and re-layouts  0.81 us (1%)
  other arithmetic  0.77 us (1%)
    all_to_all x3, blocking collectives, spread(): lax.all_to_all(value, ('row', 'col', 'seq'), 0, 0, tiled=True, axis_index...  57 us
    ppermute x4, starting transfers between devices, exchange(): return lax.ppermute(value, axis, [(n, n ^ distance) for n in range(count)])  4.69 us
    pallas_call x4, Pallas kernels, call(): pl.pallas_call(kernel, out_shape=[jax.ShapeDtypeStruct(shape, jnp.float32...  3.56 us
    ppermute x4, waiting for transfers between devices, exchange(): return lax.ppermute(value, axis, [(n, n ^ distance) for n in range(count)])  2.9 us
  transfers between devices with their start and end apart: 4, of which 4 were waited for; matrix products, arithmetic and copies ran while one was open for 1% of the time, Pallas kernels for 0%

profile of v7, /device:TPU:1, one launch (start us, length us, event | category | flops | bytes accessed | tf_op | source)
XLA Modules:
  0.0 69.9 jit_solution(10388470752291494035)
XLA Ops:
  0.0 3.2 %collective-permute-start = (f32[64,64]{1,0:T(8,128)}, f32[64,64]{1,0:T(8,128)S(1)}, u32[]{:S(2)}, u32[]{:S(2)}) collective-permute-start(f32[64,64]{1,0:T(8,128)} %bitcast.30), channel_id=1, source_target_pairs={{0,1},{1,0},{2,3},{3,2},{4,5},{5,4},{6,7},{7,6},{8,9},{9,8},{10,11... | collective-permute-start | bytes 49160 | tf_op jit(solution)/shard_map/ppermute | solution.py:207
  3.2 0.8 %broadcast_select_fusion.kept_ref = f32[64,64]{1,0:T(8,128)S(1)} fusion(f32[64,64]{1,0:T(8,128)} %bitcast.33, f32[64,64]{1,0:T(8,128)} %bitcast.31, pred[]{:T(512)S(6)} %eq.3), kind=kLoop, calls=%fused_computation | loop fusion | flops 4096 | bytes 49153 | tf_op jit(solution)/shard_map/jit(_where)/select_n | solution.py:258
  4.0 0.3 collective-permute-done.left_ref
  4.3 0.3 collective-permute-done.1.right_ref
  4.7 0.1 shard_map.127
  4.8 0.0 copy-start.8
  4.8 0.0 copy-start.9
  4.8 0.0 copy-start.10
  4.8 0.0 copy-start
  4.8 0.0 copy-start.1
  4.9 0.0 copy-start.2
  4.9 17.1 %all_to_all.33 = f32[16,64,128]{2,1,0:T(8,128)S(1)} all-to-all(f32[16,64,128]{2,1,0:T(8,128)S(1)} %bitcast.21), channel_id=1, replica_groups={{21,23,17,19,29,31,25,27,5,7,1,3,13,15,9,11},{53,55,49,51,61,63,57,59,3..., dimensions={0} | all-to-all | bytes 1048576 | tf_op jit(solution)/shard_map/all_to_all | solution.py:251
  22.0 0.6 copy-done.4
  22.7 0.0 copy-done.7
  22.7 0.1 concatenate.3.vectors_ref
  22.8 1.1 %collective-permute-done.2.other_ref = f32[1024,128]{1,0:T(8,128)S(1)} collective-permute-done((f32[1024,128]{1,0:T(8,128)S(1)}, f32[1024,128]{1,0:T(8,128)S(1)}, u32[]{:S(2)}, u32[]{:S(2)}) %collective-permute-start.2) | collective-permute-done | bytes 524320 | tf_op jit(solution)/shard_map/ppermute | solution.py:207
  23.9 1.7 %shard_map.128 = (f32[512,128]{1,0:T(8,128)S(1)}, f32[256,128]{1,0:T(8,128)S(1)}, f32[256,128]{1,0:T(8,128)S(1)}) custom-call(f32[1024,128]{1,0:T(8,128)S(1)} %bitcast.23, f32[1024,128]{1,0:T(8,128)S(1)} %collective-permute-done.2.other_ref, f32[256,128]{1,0:T(8,128)S(1)} %bitcast.29, f32[1024,128]{1,0:T(8,128)S(1)} %copy-done, f32[128,640]{1,0:T(8,128)S(1)} %copy-done.1, ...), custom_call_target="tpu_custom_call" | custom-call | tf_op jit(solution)/shard_map/pallas_call | solution.py:195
  25.6 22.9 %all_to_all.34 = f32[128,4,128]{2,1,0:T(4,128)S(1)} all-to-all(f32[128,4,128]{2,1,0:T(4,128)S(1)} %bitcast.28), channel_id=1, replica_groups={{244,246,240,242,252,254,248,250,228,230,224,226,236,238,232,234,212,21..., dimensions={0} | all-to-all | bytes 524288 | tf_op jit(solution)/shard_map/all_to_all | solution.py:251
  48.5 1.4 %collective-permute-start.3 = (f32[512,128]{1,0:T(8,128)S(1)}, f32[512,128]{1,0:T(8,128)S(1)}, u32[]{:S(2)}, u32[]{:S(2)}) collective-permute-start(f32[512,128]{1,0:T(8,128)S(1)} %bitcast.24), channel_id=1, source_target_pairs={{0,1},{1,0},{2,3},{3,2},{4,5},{5,4},{6,7},{7,6},{8,9},{9,8},{10,11... | collective-permute-start | bytes 786440 | tf_op jit(solution)/shard_map/ppermute | solution.py:207
  49.9 1.2 %collective-permute-done.3.other_ref = f32[512,128]{1,0:T(8,128)S(1)} collective-permute-done((f32[512,128]{1,0:T(8,128)S(1)}, f32[512,128]{1,0:T(8,128)S(1)}, u32[]{:S(2)}, u32[]{:S(2)}) %collective-permute-start.3) | collective-permute-done | bytes 262176 | tf_op jit(solution)/shard_map/ppermute | solution.py:207
  51.1 0.7 %shard_map.129 = f32[256,128]{1,0:T(8,128)S(1)} custom-call(f32[512,128]{1,0:T(8,128)S(1)} %bitcast.25, f32[512,128]{1,0:T(8,128)S(1)} %collective-permute-done.3.other_ref), custom_call_target="tpu_custom_call" | custom-call | tf_op jit(solution)/shard_map/pallas_call | solution.py:195
  51.8 0.0 copy-start.3
  51.8 17.0 %all_to_all.35 = f32[128,2,128]{2,1,0:T(2,128)S(1)} all-to-all(f32[128,2,128]{2,1,0:T(2,128)S(1)} %bitcast.26), channel_id=1, replica_groups={{212,214,208,210,220,222,216,218,196,198,192,194,204,206,200,202,244,24..., dimensions={0} | all-to-all | bytes 262144 | tf_op jit(solution)/shard_map/all_to_all | solution.py:251
  68.9 1.0 %shard_map.130 = f32[256,128]{1,0:T(8,128)} custom-call(f32[256,128]{1,0:T(8,128)S(1)} %bitcast.27, f32[256,128]{1,0:T(8,128)S(1)} %get-tuple-element.9.updated_ref, f32[256,128]{1,0:T(8,128)S(1)} %get-tuple-element.10.gate_ref, f32[128,128]{1,0:T(8,128)S(1)} %copy-done.3, f32[11,128]{1,0:T(8,128)S(1)} %concatenate.3.vectors_ref), custom_call_target="tpu_custom_call" | custom-call | tf_op jit(solution)/shard_map/pallas_call | solution.py:195
  (15 shorter events, 0.0 us)
Async XLA Ops:
  0.0 4.3 %collective-permute-start = (f32[64,64]{1,0:T(8,128)}, f32[64,64]{1,0:T(8,128)S(1)}, u32[]{:S(2)}, u32[]{:S(2)}) collective-permute-start(f32[64,64]{1,0:T(8,128)} %bitcast.30), channel_id=1, source_target_pairs={{0,1},{1,0},{2,3},{3,2},{4,5},{5,4},{6,7},{7,6},{8,9},{9,8},{10,11... | collective-permute-start | bytes 49160 | tf_op jit(solution)/shard_map/ppermute | solution.py:207
  3.2 1.4 %collective-permute-start.1 = (f32[64,64]{1,0:T(8,128)}, f32[64,64]{1,0:T(8,128)S(1)}, u32[]{:S(2)}, u32[]{:S(2)}) collective-permute-start(f32[64,64]{1,0:T(8,128)} %bitcast.32), channel_id=1, source_target_pairs={{0,1},{1,0},{2,3},{3,2},{4,5},{5,4},{6,7},{7,6},{8,9},{9,8},{10,11... | collective-permute-start | bytes 49160 | tf_op jit(solution)/shard_map/ppermute | solution.py:207
  4.8 17.2 %copy-start.8 = (f32[128]{0:T(128)S(1)}, f32[128]{0:T(128)}, u32[]{:S(2)}) copy-start(f32[128]{0:T(128)} %param.22) | copy-start | bytes 1540
  4.8 17.2 %copy-start.9 = (f32[128]{0:T(128)S(1)}, f32[128]{0:T(128)}, u32[]{:S(2)}) copy-start(f32[128]{0:T(128)} %param.23) | copy-start | bytes 1540
  4.8 17.2 %copy-start.10 = (f32[128]{0:T(128)S(1)}, f32[128]{0:T(128)}, u32[]{:S(2)}) copy-start(f32[128]{0:T(128)} %param.25) | copy-start | bytes 1540
  4.8 19.1 %copy-start = (f32[1024,128]{1,0:T(8,128)S(1)}, f32[1024,128]{1,0:T(8,128)}, u32[]{:S(2)}) copy-start(f32[1024,128]{1,0:T(8,128)} %mean_weight_ref.1) | copy-start | bytes 1572868
  4.8 19.1 %copy-start.1 = (f32[128,640]{1,0:T(8,128)S(1)}, f32[128,640]{1,0:T(8,128)}, u32[]{:S(2)}) copy-start(f32[128,640]{1,0:T(8,128)} %weight_ref.2) | copy-start | bytes 983044
  4.9 19.0 %copy-start.2 = (f32[32,8,128]{2,1,0:T(8,128)S(1)}, f32[32,8,128]{2,1,0:T(8,128)}, u32[]{:S(2)}) copy-start(f32[32,8,128]{2,1,0:T(8,128)} %param.13) | copy-start | bytes 393220
  22.0 1.9 %collective-permute-start.2 = (f32[1024,128]{1,0:T(8,128)S(1)}, f32[1024,128]{1,0:T(8,128)S(1)}, u32[]{:S(2)}, u32[]{:S(2)}) collective-permute-start(f32[1024,128]{1,0:T(8,128)S(1)} %bitcast.22), channel_id=1, source_target_pairs={{0,1},{1,0},{2,3},{3,2},{4,5},{5,4},{6,7},{7,6},{8,9},{9,8},{10,11... | collective-permute-start | bytes 1572872 | tf_op jit(solution)/shard_map/ppermute | solution.py:207
  22.0 0.7 copy-start.4
  22.0 0.7 copy-start.5
  22.0 0.7 copy-start.6
  22.0 0.7 copy-start.7
  48.5 2.6 %collective-permute-start.3 = (f32[512,128]{1,0:T(8,128)S(1)}, f32[512,128]{1,0:T(8,128)S(1)}, u32[]{:S(2)}, u32[]{:S(2)}) collective-permute-start(f32[512,128]{1,0:T(8,128)S(1)} %bitcast.24), channel_id=1, source_target_pairs={{0,1},{1,0},{2,3},{3,2},{4,5},{5,4},{6,7},{7,6},{8,9},{9,8},{10,11... | collective-permute-start | bytes 786440 | tf_op jit(solution)/shard_map/ppermute | solution.py:207
  51.8 17.1 %copy-start.3 = (f32[128,128]{1,0:T(8,128)S(1)}, f32[128,128]{1,0:T(8,128)}, u32[]{:S(2)}) copy-start(f32[128,128]{1,0:T(8,128)} %weight_ref.3) | copy-start | bytes 196612

commit v8 on v7

--- a/solution.py
+++ b/solution.py
@@ -67,12 +67,26 @@
         out_ref[pl.ds(n * 64, 64), :] = block
 
 
+def weights_kernel(own_ref, mean_weight_ref, weight_ref, right_ref, mean_joined_ref, joined_ref):
+    core, odd = lax.axis_index("seq"), lax.rem(lax.axis_index("col"), 2)
+    for row in range(8):
+        for q in range(4):
+            start = odd * 512 + row * 64 + q * 16 + core * 8
+            rows = pl.ds(pl.multiple_of(start, 8), 8)
+            right_ref[pl.ds((row ^ GATHER_ROW) * 32 + q * 8, 8), :] = own_ref[rows, :]
+    high, low = split(mean_weight_ref[...])
+    mean_joined_ref[...] = jnp.concatenate([high, low], axis=1)
+    high, low = split(weight_ref[...])
+    joined_ref[...] = jnp.concatenate([high, high, low], axis=0)
+
+
 def tile_kernel(
     own_ref,
     other_ref,
     pair_ref,
-    mean_weight_ref,
-    weight_ref,
+    right_ref,
+    mean_joined_ref,
+    joined_ref,
     vectors_ref,
     send_ref,
     updated_ref,
@@ -87,8 +101,9 @@
         for q in range(4):
             start = odd * 512 + row * 64 + q * 16 + core * 8
             rows = pl.ds(pl.multiple_of(start, 8), 8)
-            right_scratch[pl.ds((row ^ GATHER_ROW) * 32 + q * 8, 8), :] = jnp.where(
-                first_core, own_ref[rows, :], other_ref[rows, :]
+            target = pl.ds((row ^ GATHER_ROW) * 32 + q * 8, 8)
+            right_scratch[target, :] = jnp.where(
+                first_core, right_ref[target, :], other_ref[rows, :]
             )
     right = split(
         jnp.concatenate([right_scratch[pl.ds(j, 32, stride=8), :] for j in range(8)], axis=0)
@@ -110,16 +125,25 @@
                 high, low = split(block)
                 high_scratch[rows, columns] = high
                 low_scratch[rows, columns] = low
-    summed = product(
-        (high_scratch[...], low_scratch[...]), split(mean_weight_ref[...]), False
-    )
+    both = jnp.dot(
+        high_scratch[...], mean_joined_ref[...], preferred_element_type=jnp.float32
+    )
+    rest = jnp.dot(
+        low_scratch[...], mean_joined_ref[:, :LANES], preferred_element_type=jnp.float32
+    )
+    summed = both[:, :LANES] + (both[:, LANES:] + rest)
     pair = jnp.concatenate([pair_ref[pl.ds(j, 32, stride=8), :] for j in range(8)], axis=0)
     updated = pair + (summed + vectors_ref[0:1]) * (1.0 / SEQUENCE_COUNT)
     updated_ref[...] = updated
     center = updated - jnp.mean(updated, axis=1, keepdims=True)
     spread = jnp.mean(center * center, axis=1, keepdims=True)
     normed = center * lax.rsqrt(spread + EPSILON) * vectors_ref[1:2] + vectors_ref[2:3]
-    proj = product(split(normed), split(weight_ref[...]), False)
+    high, low = split(normed)
+    proj = jnp.dot(
+        jnp.concatenate([high, low, high], axis=1),
+        joined_ref[...],
+        preferred_element_type=jnp.float32,
+    )
     blocks = [
         proj[:, n * LANES : (n + 1) * LANES] + vectors_ref[6 + n : 7 + n] for n in range(5)
     ]
@@ -135,33 +159,32 @@
     gate_ref[...] = jax.nn.sigmoid(blocks[4])
 
 
-def triangle_kernel(own_ref, other_ref, send_ref, left_scratch, right_scratch):
-    first_core = lax.axis_index("seq") == 0
-
-    def regroup(source, part, wide):
-        return swap_groups([source(wide * 4 + r, part) for r in range(4)])
-
-    def rows_of(ref):
-        return lambda r, part: ref[pl.ds(r * 64 + part, 16, stride=4), :]
-
-    own, other = rows_of(own_ref), rows_of(other_ref)
-
-    def lower(r, part):
-        return jnp.where(first_core, own(r, part), other(r, part))
-
-    def upper(r, part):
-        return jnp.where(first_core, other(r, part), own(r, part))
-
+def regroup(ref, part, wide):
+    return swap_groups([ref[pl.ds((wide * 4 + r) * 64 + part, 16, stride=4), :] for r in range(4)])
+
+
+def regroup_kernel(own_ref, left_ref, right_ref):
     for wide in range(2):
         for part in range(2):
-            for core, source in enumerate((lower, upper)):
-                for g, block in enumerate(regroup(source, part, wide)):
-                    place = core * 8 + part * 4 + g
-                    left_scratch[wide, pl.ds(place, 16, stride=16), :] = block
-            for g, block in enumerate(regroup(own, part + 2, wide)):
-                right_scratch[wide, pl.ds((part * 4 + g) * 16, 16), :] = block
+            for g, block in enumerate(regroup(own_ref, part, wide)):
+                left_ref[pl.ds((wide * 8 + part * 4 + g) * 16, 16), :] = block
+            for g, block in enumerate(regroup(own_ref, part + 2, wide)):
+                right_ref[pl.ds((wide * 8 + part * 4 + g) * 16, 16), :] = block
+
+
+def triangle_kernel(left_ref, right_ref, other_ref, send_ref, left_scratch):
+    first_core = lax.axis_index("seq") == 0
+    for wide in range(2):
+        for part in range(2):
+            for g, other in enumerate(regroup(other_ref, part, wide)):
+                place = part * 4 + g
+                own = left_ref[pl.ds((wide * 8 + place) * 16, 16), :]
+                lower = jnp.where(first_core, own, other)
+                upper = jnp.where(first_core, other, own)
+                left_scratch[wide, pl.ds(place, 16, stride=16), :] = lower
+                left_scratch[wide, pl.ds(place + 8, 16, stride=16), :] = upper
     left = split(jnp.concatenate([left_scratch[0], left_scratch[1]], axis=1))
-    right = split(jnp.concatenate([right_scratch[0], right_scratch[1]], axis=1))
+    right = split(jnp.concatenate([right_ref[:LANES], right_ref[LANES:]], axis=1))
     mixed = product(right, left, True)
     for wide in range(2):
         for part in range(2):
@@ -275,6 +298,18 @@
         exchange(right, "seq", 1),
     )
     own = spread(blocks, gather_groups(rows, columns))
+    other = exchange(own, "seq", 1)
+    halves = pl.pallas_call(
+        weights_kernel,
+        out_shape=[
+            jax.ShapeDtypeStruct((256, LANES), jnp.float32),
+            jax.ShapeDtypeStruct((1024, 2 * LANES), jnp.bfloat16),
+            jax.ShapeDtypeStruct((3 * LANES, 5 * LANES), jnp.bfloat16),
+        ],
+        in_specs=[pl.BlockSpec(memory_space=pltpu.VMEM)] * 3,
+        out_specs=[pl.BlockSpec(memory_space=pltpu.VMEM)] * 3,
+        compiler_params=pltpu.CompilerParams(vmem_limit_bytes=VMEM_LIMIT),
+    )(own, outer_mean_weight, input_weight_matrix)
     send, updated, gate = call(
         tile_kernel,
         [(512, LANES), (256, LANES), (256, LANES)],
@@ -284,22 +319,20 @@
             pltpu.VMEM((256, 1024), jnp.bfloat16),
         ],
         own,
-        exchange(own, "seq", 1),
+        other,
         pair.reshape(256, LANES),
-        outer_mean_weight,
-        input_weight_matrix,
+        *halves,
         vectors,
     )
     own = spread(send, exchange_groups(rows, columns, OUT_ROW))
+    other = exchange(own, "seq", 1)
+    regrouped = call(regroup_kernel, [(256, LANES), (256, LANES)], [], own)
     (back,) = call(
         triangle_kernel,
         [(256, LANES)],
-        [
-            pltpu.VMEM((2, 256, LANES), jnp.float32),
-            pltpu.VMEM((2, 128, LANES), jnp.float32),
-        ],
-        own,
-        exchange(own, "seq", 1),
+        [pltpu.VMEM((2, 256, LANES), jnp.float32)],
+        *regrouped,
+        other,
     )
     mixed = spread(back, exchange_groups(rows, columns, BACK_ROW))
     (out,) = call(

time: 70.2 us -> 70.1 us (level)
    pallas_call x4 -> x5, Pallas kernels: 3.56 us -> 3.74 us  [call(): pl.pallas_call(kernel, out_shape=[jax.ShapeDtypeStruct(shape, jnp.float32...]
  transfers between devices with their start and end apart: 4 -> 4, of which waited for: 4 -> 4; matrix products, arithmetic and copies ran while one was open for 1% -> 1% of each run, Pallas kernels for 0% -> 1%
where the time goes in v8:
time: 70.1 us; the launch traced here: 69.7 us
  blocking collectives  56.9 us (81%)
  starting transfers between devices  4.84 us (7%)
  Pallas kernels  3.88 us (6%)
  waiting for transfers between devices  2.45 us (3%)
  local copies, waits for them, and re-layouts  0.81 us (1%)
  other arithmetic  0.77 us (1%)
    all_to_all x3, blocking collectives, spread(): lax.all_to_all(value, ('row', 'col', 'seq'), 0, 0, tiled=True, axis_index...  56.9 us
    ppermute x4, starting transfers between devices, exchange(): return lax.ppermute(value, axis, [(n, n ^ distance) for n in range(count)])  4.84 us
    pallas_call x5, Pallas kernels, call(): pl.pallas_call(kernel, out_shape=[jax.ShapeDtypeStruct(shape, jnp.float32...  3.74 us
    ppermute x4, waiting for transfers between devices, exchange(): return lax.ppermute(value, axis, [(n, n ^ distance) for n in range(count)])  2.45 us
  transfers between devices with their start and end apart: 4, of which 4 were waited for; matrix products, arithmetic and copies ran while one was open for 1% of the time, Pallas kernels for 1%

profile of v8, /device:TPU:1, one launch (start us, length us, event | category | flops | bytes accessed | tf_op | source)
XLA Modules:
  0.0 69.7 jit_solution(1287614224509657258)
XLA Ops:
  0.0 3.2 %collective-permute-start = (f32[64,64]{1,0:T(8,128)}, f32[64,64]{1,0:T(8,128)S(1)}, u32[]{:S(2)}, u32[]{:S(2)}) collective-permute-start(f32[64,64]{1,0:T(8,128)} %bitcast.31), channel_id=1, source_target_pairs={{0,1},{1,0},{2,3},{3,2},{4,5},{5,4},{6,7},{7,6},{8,9},{9,8},{10,11... | collective-permute-start | bytes 49160 | tf_op jit(solution)/shard_map/ppermute | solution.py:230
  3.2 0.8 %broadcast_select_fusion.kept_ref = f32[64,64]{1,0:T(8,128)S(1)} fusion(f32[64,64]{1,0:T(8,128)} %bitcast.34, f32[64,64]{1,0:T(8,128)} %bitcast.32, pred[]{:T(512)S(6)} %eq.3), kind=kLoop, calls=%fused_computation | loop fusion | flops 4096 | bytes 49153 | tf_op jit(solution)/shard_map/jit(_where)/select_n | solution.py:281
  4.0 0.3 collective-permute-done.left_ref
  4.3 0.3 collective-permute-done.1.right_ref
  4.7 0.1 shard_map.127
  4.8 0.0 copy-start.8
  4.8 0.0 copy-start.9
  4.8 0.0 copy-start.1
  4.9 17.1 %all_to_all.33 = f32[16,64,128]{2,1,0:T(8,128)S(1)} all-to-all(f32[16,64,128]{2,1,0:T(8,128)S(1)} %bitcast.24), channel_id=1, replica_groups={{21,23,17,19,29,31,25,27,5,7,1,3,13,15,9,11},{53,55,49,51,61,63,57,59,3..., dimensions={0} | all-to-all | bytes 1048576 | tf_op jit(solution)/shard_map/all_to_all | solution.py:274
  22.0 0.0 copy-start.7
  22.0 0.6 copy-done.4
  22.7 0.0 copy-done.7
  22.7 0.1 concatenate.3.vectors_ref
  22.8 0.0 copy-start.2
  22.8 0.1 shard_map.128
  23.0 0.9 %collective-permute-done.2.other_ref = f32[1024,128]{1,0:T(8,128)S(1)} collective-permute-done((f32[1024,128]{1,0:T(8,128)S(1)}, f32[1024,128]{1,0:T(8,128)S(1)}, u32[]{:S(2)}, u32[]{:S(2)}) %collective-permute-start.2) | collective-permute-done | bytes 524320 | tf_op jit(solution)/shard_map/ppermute | solution.py:230
  23.9 1.7 %shard_map.129 = (f32[512,128]{1,0:T(8,128)S(1)}, f32[256,128]{1,0:T(8,128)S(1)}, f32[256,128]{1,0:T(8,128)S(1)}) custom-call(f32[1024,128]{1,0:T(8,128)S(1)} %bitcast.23, f32[1024,128]{1,0:T(8,128)S(1)} %collective-permute-done.2.other_ref, f32[256,128]{1,0:T(8,128)S(1)} %bitcast.30, f32[256,128]{1,0:T(8,128)S(1)} %get-tuple-element.13.right_ref, ...), custom_call_target="tpu_custom_call" | custom-call | tf_op jit(solution)/shard_map/pallas_call | solution.py:218
  25.6 22.7 %all_to_all.34 = f32[128,4,128]{2,1,0:T(4,128)S(1)} all-to-all(f32[128,4,128]{2,1,0:T(4,128)S(1)} %bitcast.29), channel_id=1, replica_groups={{244,246,240,242,252,254,248,250,228,230,224,226,236,238,232,234,212,21..., dimensions={0} | all-to-all | bytes 524288 | tf_op jit(solution)/shard_map/all_to_all | solution.py:274
  48.3 1.6 %collective-permute-start.3 = (f32[512,128]{1,0:T(8,128)S(1)}, f32[512,128]{1,0:T(8,128)S(1)}, u32[]{:S(2)}, u32[]{:S(2)}) collective-permute-start(f32[512,128]{1,0:T(8,128)S(1)} %bitcast.25), channel_id=1, source_target_pairs={{0,1},{1,0},{2,3},{3,2},{4,5},{5,4},{6,7},{7,6},{8,9},{9,8},{10,11... | collective-permute-start | bytes 786440 | tf_op jit(solution)/shard_map/ppermute | solution.py:230
  49.9 0.3 shard_map.130
  50.2 0.9 %collective-permute-done.3.other_ref = f32[512,128]{1,0:T(8,128)S(1)} collective-permute-done((f32[512,128]{1,0:T(8,128)S(1)}, f32[512,128]{1,0:T(8,128)S(1)}, u32[]{:S(2)}, u32[]{:S(2)}) %collective-permute-start.3) | collective-permute-done | bytes 262176 | tf_op jit(solution)/shard_map/ppermute | solution.py:230
  51.1 0.7 shard_map.131
  51.8 17.0 %all_to_all.35 = f32[128,2,128]{2,1,0:T(2,128)S(1)} all-to-all(f32[128,2,128]{2,1,0:T(2,128)S(1)} %bitcast.27), channel_id=1, replica_groups={{212,214,208,210,220,222,216,218,196,198,192,194,204,206,200,202,244,24..., dimensions={0} | all-to-all | bytes 262144 | tf_op jit(solution)/shard_map/all_to_all | solution.py:274
  68.8 1.0 %shard_map.132 = f32[256,128]{1,0:T(8,128)} custom-call(f32[256,128]{1,0:T(8,128)S(1)} %bitcast.28, f32[256,128]{1,0:T(8,128)S(1)} %get-tuple-element.19.updated_ref, f32[256,128]{1,0:T(8,128)S(1)} %get-tuple-element.20.gate_ref, f32[128,128]{1,0:T(8,128)S(1)} %copy-done.3, f32[11,128]{1,0:T(8,128)S(1)} %concatenate.3.vectors_ref), custom_call_target="tpu_custom_call" | custom-call | tf_op jit(solution)/shard_map/pallas_call | solution.py:218
  (17 shorter events, 0.0 us)
Async XLA Ops:
  0.0 4.3 %collective-permute-start = (f32[64,64]{1,0:T(8,128)}, f32[64,64]{1,0:T(8,128)S(1)}, u32[]{:S(2)}, u32[]{:S(2)}) collective-permute-start(f32[64,64]{1,0:T(8,128)} %bitcast.31), channel_id=1, source_target_pairs={{0,1},{1,0},{2,3},{3,2},{4,5},{5,4},{6,7},{7,6},{8,9},{9,8},{10,11... | collective-permute-start | bytes 49160 | tf_op jit(solution)/shard_map/ppermute | solution.py:230
  3.2 1.4 %collective-permute-start.1 = (f32[64,64]{1,0:T(8,128)}, f32[64,64]{1,0:T(8,128)S(1)}, u32[]{:S(2)}, u32[]{:S(2)}) collective-permute-start(f32[64,64]{1,0:T(8,128)} %bitcast.33), channel_id=1, source_target_pairs={{0,1},{1,0},{2,3},{3,2},{4,5},{5,4},{6,7},{7,6},{8,9},{9,8},{10,11... | collective-permute-start | bytes 49160 | tf_op jit(solution)/shard_map/ppermute | solution.py:230
  4.8 17.2 %copy-start.8 = (f32[128]{0:T(128)S(1)}, f32[128]{0:T(128)}, u32[]{:S(2)}) copy-start(f32[128]{0:T(128)} %param.22) | copy-start | bytes 1540
  4.8 17.2 %copy-start.9 = (f32[128]{0:T(128)S(1)}, f32[128]{0:T(128)}, u32[]{:S(2)}) copy-start(f32[128]{0:T(128)} %param.23) | copy-start | bytes 1540
  4.8 17.2 %copy-start.10 = (f32[128]{0:T(128)S(1)}, f32[128]{0:T(128)}, u32[]{:S(2)}) copy-start(f32[128]{0:T(128)} %param.25) | copy-start | bytes 1540
  4.8 18.0 %copy-start = (f32[1024,128]{1,0:T(8,128)S(1)}, f32[1024,128]{1,0:T(8,128)}, u32[]{:S(2)}) copy-start(f32[1024,128]{1,0:T(8,128)} %mean_weight_ref.1) | copy-start | bytes 1572868
  4.8 18.0 %copy-start.1 = (f32[128,640]{1,0:T(8,128)S(1)}, f32[128,640]{1,0:T(8,128)}, u32[]{:S(2)}) copy-start(f32[128,640]{1,0:T(8,128)} %weight_ref.2) | copy-start | bytes 983044
  22.0 1.9 %collective-permute-start.2 = (f32[1024,128]{1,0:T(8,128)S(1)}, f32[1024,128]{1,0:T(8,128)S(1)}, u32[]{:S(2)}, u32[]{:S(2)}) collective-permute-start(f32[1024,128]{1,0:T(8,128)S(1)} %bitcast.21), channel_id=1, source_target_pairs={{0,1},{1,0},{2,3},{3,2},{4,5},{5,4},{6,7},{7,6},{8,9},{9,8},{10,11... | collective-permute-start | bytes 1572872 | tf_op jit(solution)/shard_map/ppermute | solution.py:230
  22.0 0.7 copy-start.4
  22.0 0.7 copy-start.5
  22.0 0.7 copy-start.6
  22.0 0.7 copy-start.7
  22.8 1.1 %copy-start.2 = (f32[32,8,128]{2,1,0:T(8,128)S(1)}, f32[32,8,128]{2,1,0:T(8,128)}, u32[]{:S(2)}) copy-start(f32[32,8,128]{2,1,0:T(8,128)} %param.13) | copy-start | bytes 393220
  48.3 2.8 %collective-permute-start.3 = (f32[512,128]{1,0:T(8,128)S(1)}, f32[512,128]{1,0:T(8,128)S(1)}, u32[]{:S(2)}, u32[]{:S(2)}) collective-permute-start(f32[512,128]{1,0:T(8,128)S(1)} %bitcast.25), channel_id=1, source_target_pairs={{0,1},{1,0},{2,3},{3,2},{4,5},{5,4},{6,7},{7,6},{8,9},{9,8},{10,11... | collective-permute-start | bytes 786440 | tf_op jit(solution)/shard_map/ppermute | solution.py:230
  51.7 17.0 %copy-start.3 = (f32[128,128]{1,0:T(8,128)S(1)}, f32[128,128]{1,0:T(8,128)}, u32[]{:S(2)}) copy-start(f32[128,128]{1,0:T(8,128)} %weight_ref.3) | copy-start | bytes 196612

commit v9 on v8

--- a/solution.py
+++ b/solution.py
@@ -200,7 +200,7 @@
                 send_ref[pl.ds(place * 32 + part, 16, stride=2), :] = block
 
 
-def output_kernel(mixed_ref, updated_ref, gate_ref, weight_ref, vectors_ref, out_ref):
+def output_kernel(mixed_ref, updated_ref, gate_ref, weight_ref, vectors_ref, out_ref, held_ref, semaphores):
     mixed = jnp.concatenate(
         [mixed_ref[pl.ds(0, 128, stride=2), :], mixed_ref[pl.ds(1, 128, stride=2), :]], axis=1
     )
@@ -210,8 +210,16 @@
     normed = normed * vectors_ref[3:4] + vectors_ref[4:5]
     result = product(split(normed), split(weight_ref[...]), False) + vectors_ref[5:6]
     out = updated_ref[...] + gate_ref[...] * result
-    for j in range(8):
-        out_ref[pl.ds(j, 32, stride=8), :] = out[j * 32 : (j + 1) * 32]
+    copies = []
+    for part in range(2):
+        for j in range(8):
+            begin = j * 32 + part * 16
+            held_ref[pl.ds(part * 128 + j, 16, stride=8), :] = out[begin : begin + 16]
+        rows = pl.ds(part * 128, 128)
+        copies.append(pltpu.make_async_copy(held_ref.at[rows], out_ref.at[rows], semaphores.at[part]))
+        copies[-1].start()
+    for copy in copies:
+        copy.wait()
 
 
 def call(kernel, outputs, scratch, *blocks):
@@ -335,16 +343,14 @@
         other,
     )
     mixed = spread(back, exchange_groups(rows, columns, BACK_ROW))
-    (out,) = call(
+    out = pl.pallas_call(
         output_kernel,
-        [(256, LANES)],
-        [],
-        mixed,
-        updated,
-        gate,
-        output_weight_matrix,
-        vectors,
-    )
+        out_shape=jax.ShapeDtypeStruct((256, LANES), jnp.float32),
+        in_specs=[pl.BlockSpec(memory_space=pltpu.VMEM)] * 5,
+        out_specs=pl.BlockSpec(memory_space=pltpu.HBM),
+        scratch_shapes=[pltpu.VMEM((256, LANES), jnp.float32), pltpu.SemaphoreType.DMA((2,))],
+        compiler_params=pltpu.CompilerParams(vmem_limit_bytes=VMEM_LIMIT),
+    )(mixed, updated, gate, output_weight_matrix, vectors)
     return out.reshape(pair.shape)
 
 

time: 70.1 us -> 70.1 us (level)
    pallas_call x0 -> x1, Pallas kernels: none -> 1 us  [per_device(): pl.pallas_call(output_kernel, out_shape=jax.ShapeDtypeStruct((256, LANES)...]
    pallas_call x5 -> x4, Pallas kernels: 3.74 us -> 2.76 us  [call(): pl.pallas_call(kernel, out_shape=[jax.ShapeDtypeStruct(shape, jnp.float32...]
where the time goes in v9:
time: 70.1 us; the launch traced here: 69.8 us
  blocking collectives  56.9 us (81%)
  starting transfers between devices  4.84 us (7%)
  Pallas kernels  3.89 us (6%)
  waiting for transfers between devices  2.45 us (3%)
  local copies, waits for them, and re-layouts  0.81 us (1%)
  other arithmetic  0.77 us (1%)
    all_to_all x3, blocking collectives, spread(): lax.all_to_all(value, ('row', 'col', 'seq'), 0, 0, tiled=True, axis_index...  56.9 us
    ppermute x4, starting transfers between devices, exchange(): return lax.ppermute(value, axis, [(n, n ^ distance) for n in range(count)])  4.84 us
    pallas_call x4, Pallas kernels, call(): pl.pallas_call(kernel, out_shape=[jax.ShapeDtypeStruct(shape, jnp.float32...  2.76 us
    ppermute x4, waiting for transfers between devices, exchange(): return lax.ppermute(value, axis, [(n, n ^ distance) for n in range(count)])  2.45 us
  transfers between devices with their start and end apart: 4, of which 4 were waited for; matrix products, arithmetic and copies ran while one was open for 1% of the time, Pallas kernels for 1%

profile of v9, /device:TPU:1, one launch (start us, length us, event | category | flops | bytes accessed | tf_op | source)
XLA Modules:
  0.0 69.8 jit_solution(6628546382502186329)
XLA Ops:
  0.0 3.2 %collective-permute-start = (f32[64,64]{1,0:T(8,128)}, f32[64,64]{1,0:T(8,128)S(1)}, u32[]{:S(2)}, u32[]{:S(2)}) collective-permute-start(f32[64,64]{1,0:T(8,128)} %bitcast.31), channel_id=1, source_target_pairs={{0,1},{1,0},{2,3},{3,2},{4,5},{5,4},{6,7},{7,6},{8,9},{9,8},{10,11... | collective-permute-start | bytes 49160 | tf_op jit(solution)/shard_map/ppermute | solution.py:238
  3.2 0.8 %broadcast_select_fusion.kept_ref = f32[64,64]{1,0:T(8,128)S(1)} fusion(f32[64,64]{1,0:T(8,128)} %bitcast.34, f32[64,64]{1,0:T(8,128)} %bitcast.32, pred[]{:T(512)S(6)} %eq.3), kind=kLoop, calls=%fused_computation | loop fusion | flops 4096 | bytes 49153 | tf_op jit(solution)/shard_map/jit(_where)/select_n | solution.py:289
  4.0 0.3 collective-permute-done.left_ref
  4.3 0.3 collective-permute-done.1.right_ref
  4.7 0.1 shard_map.127
  4.8 0.0 copy-start.8
  4.8 0.0 copy-start.9
  4.8 0.0 copy-start.10
  4.8 0.0 copy-start
  4.9 17.1 %all_to_all.33 = f32[16,64,128]{2,1,0:T(8,128)S(1)} all-to-all(f32[16,64,128]{2,1,0:T(8,128)S(1)} %bitcast.24), channel_id=1, replica_groups={{21,23,17,19,29,31,25,27,5,7,1,3,13,15,9,11},{53,55,49,51,61,63,57,59,3..., dimensions={0} | all-to-all | bytes 1048576 | tf_op jit(solution)/shard_map/all_to_all | solution.py:282
  22.0 0.6 copy-done.4
  22.7 0.0 copy-done.7
  22.7 0.1 concatenate.3.vectors_ref
  22.8 0.1 shard_map.128
  23.0 0.9 %collective-permute-done.2.other_ref = f32[1024,128]{1,0:T(8,128)S(1)} collective-permute-done((f32[1024,128]{1,0:T(8,128)S(1)}, f32[1024,128]{1,0:T(8,128)S(1)}, u32[]{:S(2)}, u32[]{:S(2)}) %collective-permute-start.2) | collective-permute-done | bytes 524320 | tf_op jit(solution)/shard_map/ppermute | solution.py:238
  23.9 1.7 %shard_map.129 = (f32[512,128]{1,0:T(8,128)S(1)}, f32[256,128]{1,0:T(8,128)S(1)}, f32[256,128]{1,0:T(8,128)S(1)}) custom-call(f32[1024,128]{1,0:T(8,128)S(1)} %bitcast.23, f32[1024,128]{1,0:T(8,128)S(1)} %collective-permute-done.2.other_ref, f32[256,128]{1,0:T(8,128)S(1)} %bitcast.30, f32[256,128]{1,0:T(8,128)S(1)} %get-tuple-element.13.right_ref, ...), custom_call_target="tpu_custom_call" | custom-call | tf_op jit(solution)/shard_map/pallas_call | solution.py:226
  25.6 22.7 %all_to_all.34 = f32[128,4,128]{2,1,0:T(4,128)S(1)} all-to-all(f32[128,4,128]{2,1,0:T(4,128)S(1)} %bitcast.29), channel_id=1, replica_groups={{244,246,240,242,252,254,248,250,228,230,224,226,236,238,232,234,212,21..., dimensions={0} | all-to-all | bytes 524288 | tf_op jit(solution)/shard_map/all_to_all | solution.py:282
  48.3 1.6 %collective-permute-start.3 = (f32[512,128]{1,0:T(8,128)S(1)}, f32[512,128]{1,0:T(8,128)S(1)}, u32[]{:S(2)}, u32[]{:S(2)}) collective-permute-start(f32[512,128]{1,0:T(8,128)S(1)} %bitcast.25), channel_id=1, source_target_pairs={{0,1},{1,0},{2,3},{3,2},{4,5},{5,4},{6,7},{7,6},{8,9},{9,8},{10,11... | collective-permute-start | bytes 786440 | tf_op jit(solution)/shard_map/ppermute | solution.py:238
  49.9 0.3 shard_map.130
  50.2 0.9 %collective-permute-done.3.other_ref = f32[512,128]{1,0:T(8,128)S(1)} collective-permute-done((f32[512,128]{1,0:T(8,128)S(1)}, f32[512,128]{1,0:T(8,128)S(1)}, u32[]{:S(2)}, u32[]{:S(2)}) %collective-permute-start.3) | collective-permute-done | bytes 262176 | tf_op jit(solution)/shard_map/ppermute | solution.py:238
  51.1 0.7 shard_map.131
  51.7 0.0 copy-start.3
  51.8 17.0 %all_to_all.35 = f32[128,2,128]{2,1,0:T(2,128)S(1)} all-to-all(f32[128,2,128]{2,1,0:T(2,128)S(1)} %bitcast.27), channel_id=1, replica_groups={{212,214,208,210,220,222,216,218,196,198,192,194,204,206,200,202,244,24..., dimensions={0} | all-to-all | bytes 262144 | tf_op jit(solution)/shard_map/all_to_all | solution.py:282
  68.8 1.0 %shard_map.132 = f32[256,128]{1,0:T(8,128)} custom-call(f32[256,128]{1,0:T(8,128)S(1)} %bitcast.28, f32[256,128]{1,0:T(8,128)S(1)} %get-tuple-element.19.updated_ref, f32[256,128]{1,0:T(8,128)S(1)} %get-tuple-element.20.gate_ref, f32[128,128]{1,0:T(8,128)S(1)} %copy-done.3, f32[11,128]{1,0:T(8,128)S(1)} %concatenate.3.vectors_ref), custom_call_target="tpu_custom_call" | custom-call | tf_op jit(solution)/shard_map/pallas_call | solution.py:346
  (17 shorter events, 0.0 us)
Async XLA Ops:
  0.0 4.3 %collective-permute-start = (f32[64,64]{1,0:T(8,128)}, f32[64,64]{1,0:T(8,128)S(1)}, u32[]{:S(2)}, u32[]{:S(2)}) collective-permute-start(f32[64,64]{1,0:T(8,128)} %bitcast.31), channel_id=1, source_target_pairs={{0,1},{1,0},{2,3},{3,2},{4,5},{5,4},{6,7},{7,6},{8,9},{9,8},{10,11... | collective-permute-start | bytes 49160 | tf_op jit(solution)/shard_map/ppermute | solution.py:238
  3.2 1.4 %collective-permute-start.1 = (f32[64,64]{1,0:T(8,128)}, f32[64,64]{1,0:T(8,128)S(1)}, u32[]{:S(2)}, u32[]{:S(2)}) collective-permute-start(f32[64,64]{1,0:T(8,128)} %bitcast.33), channel_id=1, source_target_pairs={{0,1},{1,0},{2,3},{3,2},{4,5},{5,4},{6,7},{7,6},{8,9},{9,8},{10,11... | collective-permute-start | bytes 49160 | tf_op jit(solution)/shard_map/ppermute | solution.py:238
  4.8 17.2 %copy-start.8 = (f32[128]{0:T(128)S(1)}, f32[128]{0:T(128)}, u32[]{:S(2)}) copy-start(f32[128]{0:T(128)} %param.22) | copy-start | bytes 1540
  4.8 17.2 %copy-start.9 = (f32[128]{0:T(128)S(1)}, f32[128]{0:T(128)}, u32[]{:S(2)}) copy-start(f32[128]{0:T(128)} %param.23) | copy-start | bytes 1540
  4.8 17.2 %copy-start.10 = (f32[128]{0:T(128)S(1)}, f32[128]{0:T(128)}, u32[]{:S(2)}) copy-start(f32[128]{0:T(128)} %param.25) | copy-start | bytes 1540
  4.8 18.0 %copy-start = (f32[1024,128]{1,0:T(8,128)S(1)}, f32[1024,128]{1,0:T(8,128)}, u32[]{:S(2)}) copy-start(f32[1024,128]{1,0:T(8,128)} %mean_weight_ref.1) | copy-start | bytes 1572868
  4.8 18.0 %copy-start.1 = (f32[128,640]{1,0:T(8,128)S(1)}, f32[128,640]{1,0:T(8,128)}, u32[]{:S(2)}) copy-start(f32[128,640]{1,0:T(8,128)} %weight_ref.2) | copy-start | bytes 983044
  22.0 1.9 %collective-permute-start.2 = (f32[1024,128]{1,0:T(8,128)S(1)}, f32[1024,128]{1,0:T(8,128)S(1)}, u32[]{:S(2)}, u32[]{:S(2)}) collective-permute-start(f32[1024,128]{1,0:T(8,128)S(1)} %bitcast.21), channel_id=1, source_target_pairs={{0,1},{1,0},{2,3},{3,2},{4,5},{5,4},{6,7},{7,6},{8,9},{9,8},{10,11... | collective-permute-start | bytes 1572872 | tf_op jit(solution)/shard_map/ppermute | solution.py:238
  22.0 0.7 copy-start.4
  22.0 0.7 copy-start.5
  22.0 0.7 copy-start.6
  22.0 0.7 copy-start.7
  22.8 1.1 %copy-start.2 = (f32[32,8,128]{2,1,0:T(8,128)S(1)}, f32[32,8,128]{2,1,0:T(8,128)}, u32[]{:S(2)}) copy-start(f32[32,8,128]{2,1,0:T(8,128)} %param.13) | copy-start | bytes 393220
  48.3 2.8 %collective-permute-start.3 = (f32[512,128]{1,0:T(8,128)S(1)}, f32[512,128]{1,0:T(8,128)S(1)}, u32[]{:S(2)}, u32[]{:S(2)}) collective-permute-start(f32[512,128]{1,0:T(8,128)S(1)} %bitcast.25), channel_id=1, source_target_pairs={{0,1},{1,0},{2,3},{3,2},{4,5},{5,4},{6,7},{7,6},{8,9},{9,8},{10,11... | collective-permute-start | bytes 786440 | tf_op jit(solution)/shard_map/ppermute | solution.py:238
  51.7 17.0 %copy-start.3 = (f32[128,128]{1,0:T(8,128)S(1)}, f32[128,128]{1,0:T(8,128)}, u32[]{:S(2)}) copy-start(f32[128,128]{1,0:T(8,128)} %weight_ref.3) | copy-start | bytes 196612
